TPU v7x, 32 devices: a whole 2x2x4 slice. The times are simulated.
32 devices in a mesh: seq: 8 (over y, x, core), head: 4 (over z).
Axes of the slice: x: 2, y: 2, z: 4, core: 2. Of those that a mesh axis runs over, the one named last changes fastest.
Arguments:
- projected: bfloat16 [12288, 6912], P(('seq', 'head')), may hold values from -10 to 10
- segment_ids: int32 [12288], replicated, may hold values from 0 to 15, never falling along the last dimension, each value on 1 to 1536 neighbouring positions
- widths: int32 [16], replicated, may hold values from 16 to 64
Outputs:
- attended: bfloat16 [12288, 2304], P(('seq', 'head'))
Inputs may be any that keep to these rules, and one draw needn't show every extreme that they name: `segment_ids`: ids never fall along the sequence; each of the 16 samples covers 1 to 1536 consecutive positions and some sample covers exactly 1536.
All inputs are finite; a program needn't handle non-finite values.
Results may differ from a plain program's by a relative error of at most 0.0088.
Values may be sent and summed in bfloat16 or wider, within the bound.
A program may use at most 128 MiB of HBM per device.

v0:
```python
import math

import jax
import jax.numpy as jnp
from jax import lax
from jax.sharding import PartitionSpec as P

D = 2304
HEADS = 24


masked_score = -1e30


def with_halo(shard, sides, width):
    for axis, dim in sides:
        size, length = (lax.axis_size(axis), shard.shape[dim])
        up = [(i, (i + 1) % size) for i in range(size - 1)]
        down = [(j, i) for i, j in up]
        last = lax.slice_in_dim(shard, length - width, length, axis=dim)
        first = lax.slice_in_dim(shard, 0, width, axis=dim)
        before = lax.ppermute(last, axis, up)
        after = lax.ppermute(first, axis, down)
        shard = jnp.concatenate([before, shard, after], axis=dim)
    return shard


def shortened(shard):

    def short(part):
        return part.astype(jnp.bfloat16) if part.dtype == jnp.float32 else part

    return jax.tree.map(short, shard)


def rotate(head_vals, row_pos, col_pos):
    quarter = head_vals.shape[-1] // 4
    frequency = 10000.0 ** (-jnp.arange(quarter, dtype=jnp.float32) / quarter)

    def turn(half_vals, place):
        angles = place.astype(jnp.float32)[:, None] * frequency[None, :]
        cosine = jnp.cos(angles)[:, None, :]
        sine_part = jnp.sin(angles)[:, None, :]
        first_half = half_vals[..., :quarter]
        second = half_vals[..., quarter:]
        return jnp.concatenate(
            [first_half * cosine - second * sine_part, first_half * sine_part + second * cosine],
            axis=-1,
        )

    middle = 2 * quarter
    return jnp.concatenate(
        [turn(head_vals[..., :middle], row_pos), turn(head_vals[..., middle:], col_pos)], axis=-1
    )


def starts_of(segment_ids):
    length = segment_ids.shape[0]
    indices = jnp.arange(length, dtype=jnp.int32)
    before = jnp.concatenate([jnp.full((1,), -1, jnp.int32), segment_ids[:-1]])
    return lax.cummax(jnp.where(segment_ids != before, indices, 0), axis=0)


def block_scores(q_rows, k_rows, q_ids, k_ids, scaling):
    scores = (
        lax.dot_general(
            q_rows, k_rows, (((1,), (1,)), ((), ())), preferred_element_type=jnp.float32
        )
        * scaling
    )
    same_seg = q_ids[:, None] == k_ids[None, :]
    return (jnp.where(same_seg, scores, masked_score), same_seg)


def dense_rows(q_rows, k_all, v_all, q_ids, k_ids, scaling):
    scores, same_seg = block_scores(q_rows, k_all, q_ids, k_ids, scaling)
    row_max = jnp.max(scores, axis=1, keepdims=True)
    weights = jnp.where(same_seg, jnp.exp(scores - row_max), 0.0)
    totals = jnp.sum(weights, axis=1, keepdims=True)
    blended = jnp.dot(weights.astype(jnp.bfloat16), v_all, preferred_element_type=jnp.float32)
    return (blended / totals).astype(jnp.bfloat16)


def attend(queries, key_rows, values, query_seg, key_seg):
    shard_rows, head_count, head_size = queries.shape
    block_rows = min(512, shard_rows)
    scaling = 1.0 / math.sqrt(head_size)

    def one_block(number):
        start_row = number * block_rows
        q_blk = lax.dynamic_slice_in_dim(queries, start_row, block_rows, 0)
        q_ids = lax.dynamic_slice_in_dim(query_seg, start_row, block_rows, 0)
        outputs = []
        for head_num in range(head_count):
            outputs.append(
                dense_rows(
                    q_blk[:, head_num],
                    key_rows[:, head_num],
                    values[:, head_num],
                    q_ids,
                    key_seg,
                    scaling,
                )
            )
        return jnp.stack(outputs, axis=1)

    results = lax.map(one_block, jnp.arange(shard_rows // block_rows, dtype=jnp.int32))
    return results.reshape(shard_rows, head_count, head_size)


def body(projected, segment_ids, widths):
    tok_dev = projected.shape[0]
    group_size = lax.axis_size("head")
    shard_rows = tok_dev * group_size
    head_size = D // HEADS
    local_heads = HEADS // group_size
    seq_index = lax.axis_index("seq")
    head_index = lax.axis_index("head")
    first_tok = (seq_index * group_size + head_index) * tok_dev
    starts = starts_of(segment_ids)
    own_seg = lax.dynamic_slice_in_dim(segment_ids, first_tok, tok_dev, 0)
    own_start = lax.dynamic_slice_in_dim(starts, first_tok, tok_dev, 0)
    offset = first_tok + jnp.arange(tok_dev, dtype=jnp.int32) - own_start
    sample_ids = jnp.arange(widths.shape[0], dtype=jnp.int32)
    width_tok = jnp.sum(
        jnp.where(own_seg[:, None] == sample_ids[None, :], widths[None, :], 0), axis=1
    )
    row_pos = offset // width_tok
    col_pos = offset % width_tok
    qkv_parts = projected.reshape(tok_dev, 3, HEADS, head_size)
    q_rot = rotate(qkv_parts[:, 0].astype(jnp.float32), row_pos, col_pos).astype(jnp.bfloat16)
    k_rot = rotate(qkv_parts[:, 1].astype(jnp.float32), row_pos, col_pos).astype(jnp.bfloat16)
    stacked = jnp.stack([q_rot, k_rot, qkv_parts[:, 2]], axis=1)
    stacked = stacked.reshape(tok_dev, 3, group_size, local_heads, head_size)
    query_seg = lax.dynamic_slice_in_dim(segment_ids, seq_index * shard_rows, shard_rows, 0)
    no_sample = jnp.full((shard_rows,), -1, jnp.int32)
    seg_pad = jnp.concatenate([no_sample, segment_ids, no_sample], axis=0)
    key_seg = lax.dynamic_slice_in_dim(seg_pad, seq_index * shard_rows, 3 * shard_rows, 0)
    qkv_part = lax.all_to_all(stacked, "head", split_axis=2, concat_axis=0, tiled=True)
    key_value = qkv_part[:, 1:]
    widened = with_halo(key_value, (("seq", 0),), qkv_part.shape[0])
    attended_heads = attend(
        qkv_part[:, 0, 0], widened[:, 0, 0], widened[:, 1, 0], query_seg, key_seg
    )
    returned = lax.all_to_all(
        shortened(attended_heads), "head", split_axis=0, concat_axis=1, tiled=True
    ).astype(attended_heads.dtype)
    return returned.reshape(tok_dev, HEADS * head_size)


def solution(mesh):
    in_specs = (P(("seq", "head"), None), P(), P())
    out_specs = P(("seq", "head"), None)
    return jax.shard_map(body, mesh=mesh, in_specs=in_specs, out_specs=out_specs, check_vma=False)
```

profile of v0, /device:TPU:3, one launch (start us, length us, event | category | flops | bytes accessed | tf_op | source)
XLA Modules:
  0.0 579.3 jit_solution(574501438986955430)
XLA Ops:
  2.5 8.0 %copy.22 = bf16[384,6912]{0,1:T(8,128)(2,1)} copy(bf16[384,6912]{1,0:T(8,128)(2,1)} %param.5) | data formatting | bytes 10616832 | tf_op args[0]
  17.2 120.8 %all_to_all.33 = bf16[384,3,4,6,96]{0,4,3,1,2:T(8,128)(2,1)S(1)} all-to-all(bf16[384,3,4,6,96]{0,4,3,1,2:T(8,128)(2,1)S(1)} %copy.23), channel_id=1, replica_groups=mesh['seq'=8,'head'=4] {'head'}, dimensions={2} | all-to-all | bytes 10616832 | tf_op jit(solution)/shard_map/all_to_all | solution.py:139
  153.1 66.4 %collective-permute-done = bf16[1536,2,1,6,96]{0,4,3,1,2:T(8,128)(2,1)} collective-permute-done((bf16[1536,2,1,6,96]{0,4,3,1,2:T(8,128)(2,1)S(1)}, bf16[1536,2,1,6,96]{0,4,3,1,2:T(8,128)(2,1)}, u32[]{:S(2)}, u32[]{:S(2)}) %collective-permute-start) | collective-permute-done | bytes 3538976 | tf_op jit(solution)/shard_map/ppermute | solution.py:22
  224.1 8.0 %pad_maximum_fusion = bf16[4608,2,1,6,96]{0,4,3,1,2:T(8,128)(2,1)} fusion(bf16[1536,2,1,6,96]{0,4,3,1,2:T(8,128)(2,1)} %collective-permute-done.1, bf16[1536,2,1,6,96]{0,4,3,1,2:T(8,128)(2,1)S(1)} %slice.153, bf16[1536,2,1,6,96]{0,4,3,1,2:T(8,128)(2,1)} %collective-permute-done), kind=kLoop, calls=%fused_computation.97 | loop fusion | flops 31850496 | bytes 21233664 | tf_op jit(solution)/shard_map/concatenate | solution.py:24
  232.0 8.7 %slice_bitcast_fusion = (bf16[4608,6,96]{0,2,1:T(8,128)(2,1)}, bf16[4608,6,96]{0,2,1:T(8,128)(2,1)}) fusion(bf16[4608,2,1,6,96]{0,4,3,1,2:T(8,128)(2,1)} %pad_maximum_fusion), kind=kLoop, calls=%fused_computation.98 | loop fusion | bytes 21233664 | tf_op jit(solution)/shard_map/squeeze | solution.py:143
  240.7 255.3 %while.10 = (s32[]{:T(128)}, bf16[3,512,6,96]{1,3,2,0:T(8,128)(2,1)}, s32[3]{0:T(128)S(1)}, s32[1536]{0:T(1024)S(1)}, s32[4608]{0:T(1024)S(1)}, /*index=5*/bf16[...) while((s32[]{:T(128)}, ...), condition=%wide.region_16.17_spmd, body=%wide.region_3.16_spmd.sunk | while | flops 5594474496 | bytes 305921152 | solution.py:107
  242.1 6.5 %fusion.183 = (f32[512]{0:T(512)S(1)}, f32[512,4608]{1,0:T(8,128)}) fusion(bf16[4608,6,96]{0,2,1:T(8,128)(2,1)} %get-tuple-element.232, bf16[1536,6,96]{0,2,1:T(8,128)(2,1)} %get-tuple-element.231, s32[]{:T(128)S(6)} %select_n.196, s32[]{:T(128)S(6)} %add.93, s32[4608]{0:T(1024)S(1)} %get-tuple-element.230, s32[512]{0:T(512)S(1)} %dynamic_slice.48), kind=kOutput, calls=%fused_computation.140.clone.1 | convolution fusion | flops 462421504 | bytes 10442760 | tf_op jit(solution)/shard_map/while/body/eval_jaxpr/dot_general | solution.py:66
  248.7 6.5 %fusion.184 = (f32[512]{0:T(512)S(1)}, f32[512,4608]{1,0:T(8,128)}) fusion(bf16[4608,6,96]{0,2,1:T(8,128)(2,1)} %get-tuple-element.232, bf16[1536,6,96]{0,2,1:T(8,128)(2,1)} %get-tuple-element.231, s32[]{:T(128)S(6)} %select_n.196, s32[]{:T(128)S(6)} %add.94, s32[4608]{0:T(1024)S(1)} %get-tuple-element.230, s32[512]{0:T(512)S(1)} %dynamic_slice.48), kind=kOutput, calls=%fused_computation.141.clone.1 | convolution fusion | flops 462421504 | bytes 10442760 | tf_op jit(solution)/shard_map/while/body/eval_jaxpr/dot_general | solution.py:66
  255.2 6.5 %fusion.185 = (f32[512]{0:T(512)S(1)}, f32[512,4608]{1,0:T(8,128)}) fusion(bf16[4608,6,96]{0,2,1:T(8,128)(2,1)} %get-tuple-element.232, bf16[1536,6,96]{0,2,1:T(8,128)(2,1)} %get-tuple-element.231, s32[]{:T(128)S(6)} %select_n.196, s32[]{:T(128)S(6)} %add.95, s32[4608]{0:T(1024)S(1)} %get-tuple-element.230, s32[512]{0:T(512)S(1)} %dynamic_slice.48), kind=kOutput, calls=%fused_computation.142.clone.1 | convolution fusion | flops 462421504 | bytes 10442760 | tf_op jit(solution)/shard_map/while/body/eval_jaxpr/dot_general | solution.py:66
  261.7 6.6 %fusion.186 = (f32[512]{0:T(512)S(1)}, f32[512,4608]{1,0:T(8,128)}) fusion(bf16[4608,6,96]{0,2,1:T(8,128)(2,1)} %get-tuple-element.232, bf16[1536,6,96]{0,2,1:T(8,128)(2,1)} %get-tuple-element.231, s32[]{:T(128)S(6)} %select_n.196, s32[]{:T(128)S(6)} %add.96, s32[4608]{0:T(1024)S(1)} %get-tuple-element.230, s32[512]{0:T(512)S(1)} %dynamic_slice.48), kind=kOutput, calls=%fused_computation.143.clone.1 | convolution fusion | flops 462421504 | bytes 10442760 | tf_op jit(solution)/shard_map/while/body/eval_jaxpr/dot_general | solution.py:66
  268.3 7.8 %fusion.187 = (f32[512]{0:T(512)S(1)}, f32[512,4608]{1,0:T(8,128)}) fusion(bf16[4608,6,96]{0,2,1:T(8,128)(2,1)} %get-tuple-element.232, bf16[1536,6,96]{0,2,1:T(8,128)(2,1)} %get-tuple-element.231, s32[]{:T(128)S(6)} %select_n.196, s32[]{:T(128)S(6)} %add.97, s32[4608]{0:T(1024)S(1)} %get-tuple-element.230, s32[512]{0:T(512)S(1)} %dynamic_slice.48), kind=kOutput, calls=%fused_computation.144.clone.1 | convolution fusion | flops 462421504 | bytes 10442760 | tf_op jit(solution)/shard_map/while/body/eval_jaxpr/dot_general | solution.py:66
  276.1 7.2 %fusion.182 = (f32[512]{0:T(512)S(1)}, f32[512,4608]{1,0:T(8,128)}) fusion(bf16[4608,6,96]{0,2,1:T(8,128)(2,1)} %get-tuple-element.232, bf16[1536,6,96]{0,2,1:T(8,128)(2,1)} %get-tuple-element.231, s32[]{:T(128)S(6)} %select_n.196, s32[4608]{0:T(1024)S(1)} %get-tuple-element.230, s32[512]{0:T(512)S(1)} %dynamic_slice.48), kind=kOutput, calls=%fused_computation.139.clone.1 | convolution fusion | flops 462421504 | bytes 10442756 | tf_op jit(solution)/shard_map/while/body/eval_jaxpr/dot_general | solution.py:66
  283.4 16.8 %fusion.188 = (f32[512]{0:T(512)S(1)}, f32[512]{0:T(512)S(1)}, f32[512]{0:T(512)S(1)}, f32[512]{0:T(512)S(1)}, f32[512]{0:T(512)S(1)}, /*index=5*/f32[512]{0:T(512)S(1)}) fusion(f32[512,4608]{1,0:T(8,128)S(1)} %bitcast.198, f32[512]{0:T(512)S(1)} %get-tuple-element.177, s32[4608]{0:T(1024)S(1)} %get-tuple-element.230, s32[512]{0:T(512)S(1)} %dynamic_slice.48, ...), kind=kLoop, calls=%fused_computation.22.clone.1 | loop fusion | flops 44823552 | bytes 56668160 | tf_op jit(solution)/shard_map/while/body/eval_jaxpr/reduce_sum | solution.py:79
  300.2 5.9 %fusion.189 = bf16[512,6,96]{0,2,1:T(8,128)(2,1)S(1)} fusion(f32[512,4608]{1,0:T(8,128)} %get-tuple-element.174, f32[512]{0:T(512)S(1)} %get-tuple-element.175, s32[4608]{0:T(1024)S(1)} %get-tuple-element.230, s32[512]{0:T(512)S(1)} %dynamic_slice.48, bf16[4608,6,96]{0,2,1:T(8,128)(2,1)} %get-tuple-element.233, f32[512]{0:T(512)S(1)} %get-tuple-element.186), kind=kOutput, calls=%fused_computation.33.clone.1 | convolution fusion | flops 462520320 | bytes 10444800 | tf_op jit(solution)/shard_map/while/body/eval_jaxpr/dot_general | solution.py:80
  316.0 5.7 fusion.193
  327.3 6.5 %fusion.183 = (f32[512]{0:T(512)S(1)}, f32[512,4608]{1,0:T(8,128)}) fusion(bf16[4608,6,96]{0,2,1:T(8,128)(2,1)} %get-tuple-element.232, bf16[1536,6,96]{0,2,1:T(8,128)(2,1)} %get-tuple-element.231, s32[]{:T(128)S(6)} %select_n.196, s32[]{:T(128)S(6)} %add.93, s32[4608]{0:T(1024)S(1)} %get-tuple-element.230, s32[512]{0:T(512)S(1)} %dynamic_slice.48), kind=kOutput, calls=%fused_computation.140.clone.1 | convolution fusion | flops 462421504 | bytes 10442760 | tf_op jit(solution)/shard_map/while/body/eval_jaxpr/dot_general | solution.py:66
  333.8 6.5 %fusion.184 = (f32[512]{0:T(512)S(1)}, f32[512,4608]{1,0:T(8,128)}) fusion(bf16[4608,6,96]{0,2,1:T(8,128)(2,1)} %get-tuple-element.232, bf16[1536,6,96]{0,2,1:T(8,128)(2,1)} %get-tuple-element.231, s32[]{:T(128)S(6)} %select_n.196, s32[]{:T(128)S(6)} %add.94, s32[4608]{0:T(1024)S(1)} %get-tuple-element.230, s32[512]{0:T(512)S(1)} %dynamic_slice.48), kind=kOutput, calls=%fused_computation.141.clone.1 | convolution fusion | flops 462421504 | bytes 10442760 | tf_op jit(solution)/shard_map/while/body/eval_jaxpr/dot_general | solution.py:66
  340.3 6.5 %fusion.185 = (f32[512]{0:T(512)S(1)}, f32[512,4608]{1,0:T(8,128)}) fusion(bf16[4608,6,96]{0,2,1:T(8,128)(2,1)} %get-tuple-element.232, bf16[1536,6,96]{0,2,1:T(8,128)(2,1)} %get-tuple-element.231, s32[]{:T(128)S(6)} %select_n.196, s32[]{:T(128)S(6)} %add.95, s32[4608]{0:T(1024)S(1)} %get-tuple-element.230, s32[512]{0:T(512)S(1)} %dynamic_slice.48), kind=kOutput, calls=%fused_computation.142.clone.1 | convolution fusion | flops 462421504 | bytes 10442760 | tf_op jit(solution)/shard_map/while/body/eval_jaxpr/dot_general | solution.py:66
  346.8 6.6 %fusion.186 = (f32[512]{0:T(512)S(1)}, f32[512,4608]{1,0:T(8,128)}) fusion(bf16[4608,6,96]{0,2,1:T(8,128)(2,1)} %get-tuple-element.232, bf16[1536,6,96]{0,2,1:T(8,128)(2,1)} %get-tuple-element.231, s32[]{:T(128)S(6)} %select_n.196, s32[]{:T(128)S(6)} %add.96, s32[4608]{0:T(1024)S(1)} %get-tuple-element.230, s32[512]{0:T(512)S(1)} %dynamic_slice.48), kind=kOutput, calls=%fused_computation.143.clone.1 | convolution fusion | flops 462421504 | bytes 10442760 | tf_op jit(solution)/shard_map/while/body/eval_jaxpr/dot_general | solution.py:66
  353.4 7.8 %fusion.187 = (f32[512]{0:T(512)S(1)}, f32[512,4608]{1,0:T(8,128)}) fusion(bf16[4608,6,96]{0,2,1:T(8,128)(2,1)} %get-tuple-element.232, bf16[1536,6,96]{0,2,1:T(8,128)(2,1)} %get-tuple-element.231, s32[]{:T(128)S(6)} %select_n.196, s32[]{:T(128)S(6)} %add.97, s32[4608]{0:T(1024)S(1)} %get-tuple-element.230, s32[512]{0:T(512)S(1)} %dynamic_slice.48), kind=kOutput, calls=%fused_computation.144.clone.1 | convolution fusion | flops 462421504 | bytes 10442760 | tf_op jit(solution)/shard_map/while/body/eval_jaxpr/dot_general | solution.py:66
  361.2 7.2 %fusion.182 = (f32[512]{0:T(512)S(1)}, f32[512,4608]{1,0:T(8,128)}) fusion(bf16[4608,6,96]{0,2,1:T(8,128)(2,1)} %get-tuple-element.232, bf16[1536,6,96]{0,2,1:T(8,128)(2,1)} %get-tuple-element.231, s32[]{:T(128)S(6)} %select_n.196, s32[4608]{0:T(1024)S(1)} %get-tuple-element.230, s32[512]{0:T(512)S(1)} %dynamic_slice.48), kind=kOutput, calls=%fused_computation.139.clone.1 | convolution fusion | flops 462421504 | bytes 10442756 | tf_op jit(solution)/shard_map/while/body/eval_jaxpr/dot_general | solution.py:66
  368.5 16.8 %fusion.188 = (f32[512]{0:T(512)S(1)}, f32[512]{0:T(512)S(1)}, f32[512]{0:T(512)S(1)}, f32[512]{0:T(512)S(1)}, f32[512]{0:T(512)S(1)}, /*index=5*/f32[512]{0:T(512)S(1)}) fusion(f32[512,4608]{1,0:T(8,128)S(1)} %bitcast.198, f32[512]{0:T(512)S(1)} %get-tuple-element.177, s32[4608]{0:T(1024)S(1)} %get-tuple-element.230, s32[512]{0:T(512)S(1)} %dynamic_slice.48, ...), kind=kLoop, calls=%fused_computation.22.clone.1 | loop fusion | flops 44823552 | bytes 56668160 | tf_op jit(solution)/shard_map/while/body/eval_jaxpr/reduce_sum | solution.py:79
  385.3 5.9 %fusion.189 = bf16[512,6,96]{0,2,1:T(8,128)(2,1)S(1)} fusion(f32[512,4608]{1,0:T(8,128)} %get-tuple-element.174, f32[512]{0:T(512)S(1)} %get-tuple-element.175, s32[4608]{0:T(1024)S(1)} %get-tuple-element.230, s32[512]{0:T(512)S(1)} %dynamic_slice.48, bf16[4608,6,96]{0,2,1:T(8,128)(2,1)} %get-tuple-element.233, f32[512]{0:T(512)S(1)} %get-tuple-element.186), kind=kOutput, calls=%fused_computation.33.clone.1 | convolution fusion | flops 462520320 | bytes 10444800 | tf_op jit(solution)/shard_map/while/body/eval_jaxpr/dot_general | solution.py:80
  412.4 6.5 %fusion.183 = (f32[512]{0:T(512)S(1)}, f32[512,4608]{1,0:T(8,128)}) fusion(bf16[4608,6,96]{0,2,1:T(8,128)(2,1)} %get-tuple-element.232, bf16[1536,6,96]{0,2,1:T(8,128)(2,1)} %get-tuple-element.231, s32[]{:T(128)S(6)} %select_n.196, s32[]{:T(128)S(6)} %add.93, s32[4608]{0:T(1024)S(1)} %get-tuple-element.230, s32[512]{0:T(512)S(1)} %dynamic_slice.48), kind=kOutput, calls=%fused_computation.140.clone.1 | convolution fusion | flops 462421504 | bytes 10442760 | tf_op jit(solution)/shard_map/while/body/eval_jaxpr/dot_general | solution.py:66
  418.9 6.5 %fusion.184 = (f32[512]{0:T(512)S(1)}, f32[512,4608]{1,0:T(8,128)}) fusion(bf16[4608,6,96]{0,2,1:T(8,128)(2,1)} %get-tuple-element.232, bf16[1536,6,96]{0,2,1:T(8,128)(2,1)} %get-tuple-element.231, s32[]{:T(128)S(6)} %select_n.196, s32[]{:T(128)S(6)} %add.94, s32[4608]{0:T(1024)S(1)} %get-tuple-element.230, s32[512]{0:T(512)S(1)} %dynamic_slice.48), kind=kOutput, calls=%fused_computation.141.clone.1 | convolution fusion | flops 462421504 | bytes 10442760 | tf_op jit(solution)/shard_map/while/body/eval_jaxpr/dot_general | solution.py:66
  425.4 6.5 %fusion.185 = (f32[512]{0:T(512)S(1)}, f32[512,4608]{1,0:T(8,128)}) fusion(bf16[4608,6,96]{0,2,1:T(8,128)(2,1)} %get-tuple-element.232, bf16[1536,6,96]{0,2,1:T(8,128)(2,1)} %get-tuple-element.231, s32[]{:T(128)S(6)} %select_n.196, s32[]{:T(128)S(6)} %add.95, s32[4608]{0:T(1024)S(1)} %get-tuple-element.230, s32[512]{0:T(512)S(1)} %dynamic_slice.48), kind=kOutput, calls=%fused_computation.142.clone.1 | convolution fusion | flops 462421504 | bytes 10442760 | tf_op jit(solution)/shard_map/while/body/eval_jaxpr/dot_general | solution.py:66
  431.9 6.6 %fusion.186 = (f32[512]{0:T(512)S(1)}, f32[512,4608]{1,0:T(8,128)}) fusion(bf16[4608,6,96]{0,2,1:T(8,128)(2,1)} %get-tuple-element.232, bf16[1536,6,96]{0,2,1:T(8,128)(2,1)} %get-tuple-element.231, s32[]{:T(128)S(6)} %select_n.196, s32[]{:T(128)S(6)} %add.96, s32[4608]{0:T(1024)S(1)} %get-tuple-element.230, s32[512]{0:T(512)S(1)} %dynamic_slice.48), kind=kOutput, calls=%fused_computation.143.clone.1 | convolution fusion | flops 462421504 | bytes 10442760 | tf_op jit(solution)/shard_map/while/body/eval_jaxpr/dot_general | solution.py:66
  438.5 7.8 %fusion.187 = (f32[512]{0:T(512)S(1)}, f32[512,4608]{1,0:T(8,128)}) fusion(bf16[4608,6,96]{0,2,1:T(8,128)(2,1)} %get-tuple-element.232, bf16[1536,6,96]{0,2,1:T(8,128)(2,1)} %get-tuple-element.231, s32[]{:T(128)S(6)} %select_n.196, s32[]{:T(128)S(6)} %add.97, s32[4608]{0:T(1024)S(1)} %get-tuple-element.230, s32[512]{0:T(512)S(1)} %dynamic_slice.48), kind=kOutput, calls=%fused_computation.144.clone.1 | convolution fusion | flops 462421504 | bytes 10442760 | tf_op jit(solution)/shard_map/while/body/eval_jaxpr/dot_general | solution.py:66
  446.4 7.2 %fusion.182 = (f32[512]{0:T(512)S(1)}, f32[512,4608]{1,0:T(8,128)}) fusion(bf16[4608,6,96]{0,2,1:T(8,128)(2,1)} %get-tuple-element.232, bf16[1536,6,96]{0,2,1:T(8,128)(2,1)} %get-tuple-element.231, s32[]{:T(128)S(6)} %select_n.196, s32[4608]{0:T(1024)S(1)} %get-tuple-element.230, s32[512]{0:T(512)S(1)} %dynamic_slice.48), kind=kOutput, calls=%fused_computation.139.clone.1 | convolution fusion | flops 462421504 | bytes 10442756 | tf_op jit(solution)/shard_map/while/body/eval_jaxpr/dot_general | solution.py:66
  453.6 16.8 %fusion.188 = (f32[512]{0:T(512)S(1)}, f32[512]{0:T(512)S(1)}, f32[512]{0:T(512)S(1)}, f32[512]{0:T(512)S(1)}, f32[512]{0:T(512)S(1)}, /*index=5*/f32[512]{0:T(512)S(1)}) fusion(f32[512,4608]{1,0:T(8,128)S(1)} %bitcast.198, f32[512]{0:T(512)S(1)} %get-tuple-element.177, s32[4608]{0:T(1024)S(1)} %get-tuple-element.230, s32[512]{0:T(512)S(1)} %dynamic_slice.48, ...), kind=kLoop, calls=%fused_computation.22.clone.1 | loop fusion | flops 44823552 | bytes 56668160 | tf_op jit(solution)/shard_map/while/body/eval_jaxpr/reduce_sum | solution.py:79
  470.4 5.9 %fusion.189 = bf16[512,6,96]{0,2,1:T(8,128)(2,1)S(1)} fusion(f32[512,4608]{1,0:T(8,128)} %get-tuple-element.174, f32[512]{0:T(512)S(1)} %get-tuple-element.175, s32[4608]{0:T(1024)S(1)} %get-tuple-element.230, s32[512]{0:T(512)S(1)} %dynamic_slice.48, bf16[4608,6,96]{0,2,1:T(8,128)(2,1)} %get-tuple-element.233, f32[512]{0:T(512)S(1)} %get-tuple-element.186), kind=kOutput, calls=%fused_computation.33.clone.1 | convolution fusion | flops 462520320 | bytes 10444800 | tf_op jit(solution)/shard_map/while/body/eval_jaxpr/dot_general | solution.py:80
  499.4 73.3 %all_to_all.34 = bf16[1536,6,96]{2,1,0:T(8,128)(2,1)} all-to-all(bf16[1536,6,96]{2,1,0:T(8,128)(2,1)S(1)} %bitcast.207), channel_id=1, replica_groups=mesh['seq'=8,'head'=4] {'head'}, dimensions={0} | all-to-all | bytes 3538944 | tf_op jit(solution)/shard_map/all_to_all | solution.py:145
  (141 shorter events, 93.9 us)
Async XLA Ops:
  141.5 78.0 %collective-permute-start = (bf16[1536,2,1,6,96]{0,4,3,1,2:T(8,128)(2,1)S(1)}, bf16[1536,2,1,6,96]{0,4,3,1,2:T(8,128)(2,1)}, u32[]{:S(2)}, u32[]{:S(2)}) collective-permute-start(bf16[1536,2,1,6,96]{0,4,3,1,2:T(8,128)(2,1)S(1)} %slice.153), channel_id=1, source_target_pairs={{0,4},{4,8},{8,12},{12,16},{16,20},{20,24},{24,28},{1,5},{5,9},{9,... | collective-permute-start | bytes 10616840 | tf_op jit(solution)/shard_map/ppermute | solution.py:22
  146.0 78.1 %collective-permute-start.1 = (bf16[1536,2,1,6,96]{0,4,3,1,2:T(8,128)(2,1)S(1)}, bf16[1536,2,1,6,96]{0,4,3,1,2:T(8,128)(2,1)}, u32[]{:S(2)}, u32[]{:S(2)}) collective-permute-start(bf16[1536,2,1,6,96]{0,4,3,1,2:T(8,128)(2,1)S(1)} %slice.153), channel_id=1, source_target_pairs={{4,0},{8,4},{12,8},{16,12},{20,16},{24,20},{28,24},{5,1},{9,5},{13... | collective-permute-start | bytes 10616840 | tf_op jit(solution)/shard_map/ppermute | solution.py:23
  232.0 8.7 %copy-start.2 = (s32[4608]{0:T(1024)S(1)}, s32[4608]{0:T(1024)}, u32[]{:S(2)}) copy-start(s32[4608]{0:T(1024)} %fusion.135) | copy-start | bytes 55300
  240.7 14.5 %copy-start.3 = (s32[1536]{0:T(1024)}, s32[1536]{0:T(1024)S(1)}, u32[]{:S(2)}) copy-start(s32[1536]{0:T(1024)S(1)} %get-tuple-element.229) | copy-start | bytes 18436 | tf_op jit(solution)/shard_map/while
  268.3 15.1 %slice-start = ((s8[9437184]{0:T(1024)(128)(4,1)}), s8[4194304]{0:T(1024)(128)(4,1)S(1)}, s32[]{:S(2)}) async-start(s8[9437184]{0:T(1024)(128)(4,1)} %bitcast.197), calls=%async_computation.2 | async-start | bytes 8388608 | tf_op jit(solution)/shard_map/while
  268.3 15.1 %slice-start.1 = ((s8[9437184]{0:T(1024)(128)(4,1)}), s8[4194304]{0:T(1024)(128)(4,1)S(1)}, s32[]{:S(2)}) async-start(s8[9437184]{0:T(1024)(128)(4,1)} %bitcast.197), calls=%async_computation.3 | async-start | bytes 8388608 | tf_op jit(solution)/shard_map/while
  268.3 15.1 %copy-start = (f32[512,4608]{1,0:T(8,128)S(1)}, f32[512,4608]{1,0:T(8,128)}, u32[]{:S(2)}) copy-start(f32[512,4608]{1,0:T(8,128)} %get-tuple-element.178) | copy-start | bytes 28311556 | tf_op jit(solution)/shard_map/while
  276.1 7.3 %slice-start.2 = ((s8[9437184]{0:T(1024)(128)(4,1)}), s8[1048576]{0:T(1024)(128)(4,1)S(1)}, s32[]{:S(2)}) async-start(s8[9437184]{0:T(1024)(128)(4,1)} %bitcast.197), calls=%async_computation.4 | async-start | bytes 2097152 | tf_op jit(solution)/shard_map/while
  300.2 9.3 %slice-start.3 = ((s8[9437184]{0:T(1024)(128)(4,1)}), s8[4194304]{0:T(1024)(128)(4,1)S(1)}, s32[]{:S(2)}) async-start(s8[9437184]{0:T(1024)(128)(4,1)} %bitcast.199), calls=%async_computation.5 | async-start | bytes 8388608 | tf_op jit(solution)/shard_map/while
  300.2 9.3 %slice-start.4 = ((s8[9437184]{0:T(1024)(128)(4,1)}), s8[4194304]{0:T(1024)(128)(4,1)S(1)}, s32[]{:S(2)}) async-start(s8[9437184]{0:T(1024)(128)(4,1)} %bitcast.199), calls=%async_computation.6 | async-start | bytes 8388608 | tf_op jit(solution)/shard_map/while
  306.1 6.6 %slice-start.6 = ((s8[9437184]{0:T(1024)(128)(4,1)}), s8[4194304]{0:T(1024)(128)(4,1)S(1)}, s32[]{:S(2)}) async-start(s8[9437184]{0:T(1024)(128)(4,1)} %bitcast.201), calls=%async_computation.8 | async-start | bytes 8388608 | tf_op jit(solution)/shard_map/while
  306.1 6.6 %slice-start.7 = ((s8[9437184]{0:T(1024)(128)(4,1)}), s8[1048576]{0:T(1024)(128)(4,1)S(1)}, s32[]{:S(2)}) async-start(s8[9437184]{0:T(1024)(128)(4,1)} %bitcast.201), calls=%async_computation.9 | async-start | bytes 2097152 | tf_op jit(solution)/shard_map/while
  321.7 4.1 copy-start.4
  325.8 14.5 %copy-start.3 = (s32[1536]{0:T(1024)}, s32[1536]{0:T(1024)S(1)}, u32[]{:S(2)}) copy-start(s32[1536]{0:T(1024)S(1)} %get-tuple-element.229) | copy-start | bytes 18436 | tf_op jit(solution)/shard_map/while
  353.4 15.1 %slice-start = ((s8[9437184]{0:T(1024)(128)(4,1)}), s8[4194304]{0:T(1024)(128)(4,1)S(1)}, s32[]{:S(2)}) async-start(s8[9437184]{0:T(1024)(128)(4,1)} %bitcast.197), calls=%async_computation.2 | async-start | bytes 8388608 | tf_op jit(solution)/shard_map/while
  353.4 15.1 %slice-start.1 = ((s8[9437184]{0:T(1024)(128)(4,1)}), s8[4194304]{0:T(1024)(128)(4,1)S(1)}, s32[]{:S(2)}) async-start(s8[9437184]{0:T(1024)(128)(4,1)} %bitcast.197), calls=%async_computation.3 | async-start | bytes 8388608 | tf_op jit(solution)/shard_map/while
  353.4 15.1 %copy-start = (f32[512,4608]{1,0:T(8,128)S(1)}, f32[512,4608]{1,0:T(8,128)}, u32[]{:S(2)}) copy-start(f32[512,4608]{1,0:T(8,128)} %get-tuple-element.178) | copy-start | bytes 28311556 | tf_op jit(solution)/shard_map/while
  361.2 7.3 %slice-start.2 = ((s8[9437184]{0:T(1024)(128)(4,1)}), s8[1048576]{0:T(1024)(128)(4,1)S(1)}, s32[]{:S(2)}) async-start(s8[9437184]{0:T(1024)(128)(4,1)} %bitcast.197), calls=%async_computation.4 | async-start | bytes 2097152 | tf_op jit(solution)/shard_map/while
  385.3 9.3 %slice-start.3 = ((s8[9437184]{0:T(1024)(128)(4,1)}), s8[4194304]{0:T(1024)(128)(4,1)S(1)}, s32[]{:S(2)}) async-start(s8[9437184]{0:T(1024)(128)(4,1)} %bitcast.199), calls=%async_computation.5 | async-start | bytes 8388608 | tf_op jit(solution)/shard_map/while
  385.3 9.3 %slice-start.4 = ((s8[9437184]{0:T(1024)(128)(4,1)}), s8[4194304]{0:T(1024)(128)(4,1)S(1)}, s32[]{:S(2)}) async-start(s8[9437184]{0:T(1024)(128)(4,1)} %bitcast.199), calls=%async_computation.6 | async-start | bytes 8388608 | tf_op jit(solution)/shard_map/while
  391.2 6.6 %slice-start.6 = ((s8[9437184]{0:T(1024)(128)(4,1)}), s8[4194304]{0:T(1024)(128)(4,1)S(1)}, s32[]{:S(2)}) async-start(s8[9437184]{0:T(1024)(128)(4,1)} %bitcast.201), calls=%async_computation.8 | async-start | bytes 8388608 | tf_op jit(solution)/shard_map/while
  391.2 6.6 %slice-start.7 = ((s8[9437184]{0:T(1024)(128)(4,1)}), s8[1048576]{0:T(1024)(128)(4,1)S(1)}, s32[]{:S(2)}) async-start(s8[9437184]{0:T(1024)(128)(4,1)} %bitcast.201), calls=%async_computation.9 | async-start | bytes 2097152 | tf_op jit(solution)/shard_map/while
  406.8 4.1 copy-start.4
  410.9 14.5 %copy-start.3 = (s32[1536]{0:T(1024)}, s32[1536]{0:T(1024)S(1)}, u32[]{:S(2)}) copy-start(s32[1536]{0:T(1024)S(1)} %get-tuple-element.229) | copy-start | bytes 18436 | tf_op jit(solution)/shard_map/while
  438.5 15.1 %slice-start = ((s8[9437184]{0:T(1024)(128)(4,1)}), s8[4194304]{0:T(1024)(128)(4,1)S(1)}, s32[]{:S(2)}) async-start(s8[9437184]{0:T(1024)(128)(4,1)} %bitcast.197), calls=%async_computation.2 | async-start | bytes 8388608 | tf_op jit(solution)/shard_map/while
  438.5 15.1 %slice-start.1 = ((s8[9437184]{0:T(1024)(128)(4,1)}), s8[4194304]{0:T(1024)(128)(4,1)S(1)}, s32[]{:S(2)}) async-start(s8[9437184]{0:T(1024)(128)(4,1)} %bitcast.197), calls=%async_computation.3 | async-start | bytes 8388608 | tf_op jit(solution)/shard_map/while
  438.5 15.1 %copy-start = (f32[512,4608]{1,0:T(8,128)S(1)}, f32[512,4608]{1,0:T(8,128)}, u32[]{:S(2)}) copy-start(f32[512,4608]{1,0:T(8,128)} %get-tuple-element.178) | copy-start | bytes 28311556 | tf_op jit(solution)/shard_map/while
  446.4 7.3 %slice-start.2 = ((s8[9437184]{0:T(1024)(128)(4,1)}), s8[1048576]{0:T(1024)(128)(4,1)S(1)}, s32[]{:S(2)}) async-start(s8[9437184]{0:T(1024)(128)(4,1)} %bitcast.197), calls=%async_computation.4 | async-start | bytes 2097152 | tf_op jit(solution)/shard_map/while
  470.4 9.3 %slice-start.3 = ((s8[9437184]{0:T(1024)(128)(4,1)}), s8[4194304]{0:T(1024)(128)(4,1)S(1)}, s32[]{:S(2)}) async-start(s8[9437184]{0:T(1024)(128)(4,1)} %bitcast.199), calls=%async_computation.5 | async-start | bytes 8388608 | tf_op jit(solution)/shard_map/while
  470.4 9.3 %slice-start.4 = ((s8[9437184]{0:T(1024)(128)(4,1)}), s8[4194304]{0:T(1024)(128)(4,1)S(1)}, s32[]{:S(2)}) async-start(s8[9437184]{0:T(1024)(128)(4,1)} %bitcast.199), calls=%async_computation.6 | async-start | bytes 8388608 | tf_op jit(solution)/shard_map/while
  476.3 6.6 %slice-start.6 = ((s8[9437184]{0:T(1024)(128)(4,1)}), s8[4194304]{0:T(1024)(128)(4,1)S(1)}, s32[]{:S(2)}) async-start(s8[9437184]{0:T(1024)(128)(4,1)} %bitcast.201), calls=%async_computation.8 | async-start | bytes 8388608 | tf_op jit(solution)/shard_map/while
  476.3 6.6 %slice-start.7 = ((s8[9437184]{0:T(1024)(128)(4,1)}), s8[1048576]{0:T(1024)(128)(4,1)S(1)}, s32[]{:S(2)}) async-start(s8[9437184]{0:T(1024)(128)(4,1)} %bitcast.201), calls=%async_computation.9 | async-start | bytes 2097152 | tf_op jit(solution)/shard_map/while
  (9 other events, 30.0 us)
where the time goes:
time: 581 us; the launch traced here: 579 us
  matrix products  197 us (34%)
  blocking collectives  194 us (33%)
  waiting for transfers between devices  71 us (12%)
  other arithmetic  67.3 us (12%)
  local copies, waits for them, and re-layouts  40.3 us (7%)
  starting transfers between devices  6.44 us (1%)
    dot_general x18, matrix products, block_scores(): lax.dot_general(q_rows, k_rows, (((1,), (1,)), ((), ())), preferred_eleme...  124 us
    all_to_all x1, blocking collectives, body(): lax.all_to_all(stacked, 'head', split_axis=2, concat_axis=0, tiled=True)  121 us
    dot_general x18, matrix products, dense_rows(): jnp.dot(weights.astype(jnp.bfloat16), v_all, preferred_element_type=jnp.f...  73.6 us
    all_to_all x1, blocking collectives, body(): lax.all_to_all(shortened(attended_heads), 'head', split_axis=0, concat_ax...  73.3 us
    ppermute x1, waiting for transfers between devices, with_halo(): before = lax.ppermute(last, axis, up)  66.4 us
    reduce_sum x3, other arithmetic, dense_rows(): totals = jnp.sum(weights, axis=1, keepdims=True)  50.4 us
  transfers between devices with their start and end apart: 2, of which 2 were waited for; matrix products, arithmetic and copies ran while one was open for 1% of the time, Pallas kernels for 0%

commit v1 on v0

v1 whole, which is shorter than its diff:
```python
import functools
import math

import jax
import jax.numpy as jnp
from jax import lax
from jax.experimental import pallas as pl
from jax.experimental.pallas import tpu as pltpu
from jax.sharding import PartitionSpec as P

D = 2304
HEADS = 24
HEAD = D // HEADS
QUARTER = HEAD // 4
ONES = 16
APART = -131072.0
MESH = pl.DeviceIdType.MESH


def transposed(block):
    return jnp.transpose(block.astype(jnp.float32), (1, 0))


def kernel(
    group, chunks, seqs, x_ref, turns_ref, kaug_ref, qaug_ref, out_ref,
    send, held, keys, blended, back,
    in_send, in_recv, in_own, halo_send, halo_recv, back_send, back_recv, back_own,
):
    tok = x_ref.shape[0]
    span = group * HEAD
    aug = kaug_ref.shape[1]
    seq = lax.axis_index("seq")
    me = lax.axis_index("head")
    has_left = seq > 0
    has_right = seq < seqs - 1
    scale = math.log2(math.e) / math.sqrt(HEAD)

    barrier = pltpu.get_barrier_semaphore()
    for d in range(1, group):
        pl.semaphore_signal(
            barrier, inc=1, device_id={"head": lax.rem(me + d, group)}, device_id_type=MESH
        )

    @pl.when(has_left)
    def _():
        pl.semaphore_signal(barrier, inc=1, device_id={"seq": seq - 1}, device_id_type=MESH)

    @pl.when(has_right)
    def _():
        pl.semaphore_signal(barrier, inc=1, device_id={"seq": seq + 1}, device_id_type=MESH)

    pl.semaphore_wait(
        barrier, group - 1 + has_left.astype(jnp.int32) + has_right.astype(jnp.int32)
    )

    def in_copy(j, d):
        dest = lax.rem(me + d, group)
        return pltpu.make_async_remote_copy(
            src_ref=send.at[j, dest],
            dst_ref=held.at[j, group + me],
            send_sem=in_send.at[j, d - 1],
            recv_sem=in_recv.at[j, d - 1],
            device_id={"head": dest},
            device_id_type=MESH,
        )

    def own_copy(j):
        return pltpu.make_async_copy(send.at[j, me], held.at[j, group + me], in_own.at[j])

    def halo_copy(j, side):
        slot = 0 if side == 0 else 2 * group
        return pltpu.make_async_remote_copy(
            src_ref=held.at[j, pl.ds(group, group), pl.ds(1, 2)],
            dst_ref=held.at[j, pl.ds(slot, group), pl.ds(1, 2)],
            send_sem=halo_send.at[j, side],
            recv_sem=halo_recv.at[j, side],
            device_id={"seq": seq + 1 if side == 0 else seq - 1},
            device_id_type=MESH,
        )

    def back_copy(j, d):
        dest = lax.rem(me + d, group)
        return pltpu.make_async_remote_copy(
            src_ref=blended.at[j, dest],
            dst_ref=back.at[j, me],
            send_sem=back_send.at[j, d - 1],
            recv_sem=back_recv.at[j, d - 1],
            device_id={"head": dest},
            device_id_type=MESH,
        )

    def back_own_copy(j):
        return pltpu.make_async_copy(blended.at[j, me], back.at[j, me], back_own.at[j])

    def issue(j):
        for part in range(3):
            first = pl.multiple_of(part * D + j * span, 128)
            cols = transposed(x_ref[:, pl.ds(first, span)])
            for z in range(group):
                vals = cols[z * HEAD:(z + 1) * HEAD]
                if part < 2:
                    pieces = []
                    for half in range(2):
                        cosine, sine = turns_ref[2 * half], turns_ref[2 * half + 1]
                        low = vals[2 * half * QUARTER:(2 * half + 1) * QUARTER]
                        high = vals[(2 * half + 1) * QUARTER:(2 * half + 2) * QUARTER]
                        pieces += [low * cosine - high * sine, low * sine + high * cosine]
                    vals = jnp.concatenate(pieces, axis=0)
                send[j, z, part] = vals.astype(jnp.bfloat16)
        for d in range(1, group):
            in_copy(j, d).start()
        own_copy(j).start()

    def arrive(j):
        own_copy(j).wait()
        for d in range(1, group):
            in_copy(j, d).wait_recv()

        @pl.when(has_right)
        def _():
            halo_copy(j, 0).start()

        @pl.when(has_left)
        def _():
            halo_copy(j, 1).start()

    def halo_arrive(j):
        @pl.when(has_left)
        def _():
            halo_copy(j, 0).wait_recv()

        @pl.when(has_right)
        def _():
            halo_copy(j, 1).wait_recv()

        @pl.when(jnp.logical_not(has_left))
        def _():
            for z in range(group):
                held[j, z] = jnp.zeros((3, HEAD, tok), jnp.bfloat16)

        @pl.when(jnp.logical_not(has_right))
        def _():
            for z in range(group):
                held[j, 2 * group + z] = jnp.zeros((3, HEAD, tok), jnp.bfloat16)

    window = 2 * group + 1
    several = 3 if window % 3 == 0 else 1

    def attend(j):
        def lay(slot, carry):
            joined = jnp.concatenate([held[j, slot, 1], kaug_ref[slot]], axis=0)
            keys[slot] = transposed(joined).astype(jnp.bfloat16)
            return carry

        lax.fori_loop(0, 3 * group, lay, 0)
        ones = jnp.ones((ONES, tok), jnp.bfloat16)

        def query_block(i, carry):
            q = jnp.concatenate([held[j, group + i, 0], qaug_ref[i]], axis=0)

            def key_blocks(step, state):
                top, acc = state
                scores = []
                for b in range(several):
                    scores.append(
                        jnp.dot(keys[i + step * several + b], q, preferred_element_type=jnp.float32)
                    )
                new_top = top
                for s in scores:
                    new_top = jnp.maximum(new_top, jnp.max(s, axis=0, keepdims=True))
                acc = acc * jnp.exp2((top - new_top) * scale)
                for b, s in enumerate(scores):
                    weights = jnp.exp2((s - new_top) * scale).astype(jnp.bfloat16)
                    v = jnp.concatenate([held[j, i + step * several + b, 2], ones], axis=0)
                    acc = acc + jnp.dot(v, weights, preferred_element_type=jnp.float32)
                return new_top, acc

            top = jnp.full((1, tok), -1e30, jnp.float32)
            acc = jnp.zeros((HEAD + ONES, tok), jnp.float32)
            top, acc = lax.fori_loop(0, window // several, key_blocks, (top, acc))
            blended[j, i] = (acc[:HEAD] / acc[HEAD:HEAD + 1]).astype(jnp.bfloat16)
            return carry

        lax.fori_loop(0, group, query_block, 0)
        for d in range(1, group):
            back_copy(j, d).start()
        back_own_copy(j).start()

    issue(0)

    def step(t, carry):
        @pl.when(t + 1 < chunks)
        def _():
            issue(t + 1)

        @pl.when(t < chunks)
        def _():
            arrive(t)

        @pl.when(t >= 1)
        def _():
            halo_arrive(t - 1)
            attend(t - 1)

        return carry

    lax.fori_loop(0, chunks + 1, step, 0)

    def finish(j, carry):
        back_own_copy(j).wait()
        for d in range(1, group):
            back_copy(j, d).wait_recv()
        rows = jnp.concatenate([back[j, z] for z in range(group)], axis=0)
        out_ref[:, pl.ds(pl.multiple_of(j * span, 128), span)] = transposed(rows).astype(
            jnp.bfloat16
        )
        for d in range(1, group):
            in_copy(j, d).wait_send()
            back_copy(j, d).wait_send()

        @pl.when(has_right)
        def _():
            halo_copy(j, 0).wait_send()

        @pl.when(has_left)
        def _():
            halo_copy(j, 1).wait_send()

        return carry

    lax.fori_loop(0, chunks, finish, 0)


def body(projected, segment_ids, widths):
    tok = projected.shape[0]
    group = lax.axis_size("head")
    seqs = lax.axis_size("seq")
    chunks = HEADS // group
    shard = tok * group
    seq = lax.axis_index("seq")
    first = (seq * group + lax.axis_index("head")) * tok
    ids = jnp.arange(widths.shape[0], dtype=jnp.int32)

    starts = jnp.sum((segment_ids[None, :] < ids[:, None]).astype(jnp.int32), axis=1)
    own = lax.dynamic_slice_in_dim(segment_ids, first, tok, 0)
    mine = own[None, :] == ids[:, None]
    own_start = jnp.sum(jnp.where(mine, starts[:, None], 0), axis=0)
    width = jnp.sum(jnp.where(mine, widths[:, None], 0), axis=0)
    offset = first + jnp.arange(tok, dtype=jnp.int32) - own_start
    row_pos = offset // width
    col_pos = offset - row_pos * width
    frequency = 10000.0 ** (-jnp.arange(QUARTER, dtype=jnp.float32) / QUARTER)
    places = jnp.stack([row_pos, col_pos]).astype(jnp.float32)
    angles = places[:, None, :] * frequency[None, :, None]
    turns = jnp.stack([jnp.cos(angles), jnp.sin(angles)], axis=1).reshape(4, QUARTER, tok)

    count = widths.shape[0]
    aug = -(-(HEAD + count + 1) // 128) * 128 - HEAD
    none = jnp.full((shard,), count, jnp.int32)
    padded = jnp.concatenate([none, segment_ids, none])
    key_seg = lax.dynamic_slice_in_dim(padded, seq * shard, 3 * shard, 0)
    lanes = jnp.arange(aug, dtype=jnp.int32)[None, :, None]
    key_seg = key_seg.reshape(3 * group, 1, tok)
    kaug = (key_seg == lanes).astype(jnp.bfloat16)
    query_seg = key_seg[group:2 * group]
    qaug = jnp.where((query_seg == lanes) | (lanes > count), 0.0, APART).astype(jnp.bfloat16)

    vmem = pl.BlockSpec(memory_space=pltpu.VMEM)
    dma = pltpu.SemaphoreType.DMA
    return pl.pallas_call(
        functools.partial(kernel, group, chunks, seqs),
        out_shape=jax.ShapeDtypeStruct((tok, D), jnp.bfloat16),
        in_specs=[vmem] * 4,
        out_specs=vmem,
        scratch_shapes=[
            pltpu.VMEM((chunks, group, 3, HEAD, tok), jnp.bfloat16),
            pltpu.VMEM((chunks, 3 * group, 3, HEAD, tok), jnp.bfloat16),
            pltpu.VMEM((3 * group, tok, HEAD + aug), jnp.bfloat16),
            pltpu.VMEM((chunks, group, HEAD, tok), jnp.bfloat16),
            pltpu.VMEM((chunks, group, HEAD, tok), jnp.bfloat16),
            dma((chunks, group - 1)),
            dma((chunks, group - 1)),
            dma((chunks,)),
            dma((chunks, 2)),
            dma((chunks, 2)),
            dma((chunks, group - 1)),
            dma((chunks, group - 1)),
            dma((chunks,)),
        ],
        compiler_params=pltpu.CompilerParams(
            collective_id=0, has_side_effects=True, vmem_limit_bytes=56 * 2**20
        ),
        cost_estimate=pl.CostEstimate(
            flops=4 * shard * shard * 2 * D // group, bytes_accessed=tok * D * 8, transcendentals=0
        ),
    )(projected, turns, kaug, qaug)


def solution(mesh):
    in_specs = (P(("seq", "head"), None), P(), P())
    out_specs = P(("seq", "head"), None)
    return jax.shard_map(body, mesh=mesh, in_specs=in_specs, out_specs=out_specs, check_vma=False)
```

time: 581 us -> 197 us (0.34)
  the two profiles are of different devices: /device:TPU:3 before, /device:TPU:0 now
where the time goes in v1:
time: 197 us
  Pallas kernels  188 us (95%)
  other arithmetic  5.29 us (3%)
  local copies, waits for them, and re-layouts  3.6 us (2%)
    pallas_call x1, Pallas kernels, body(): pl.pallas_call(functools.partial(kernel, group, chunks, seqs), out_shape=...  188 us

profile of v1, /device:TPU:0, one launch (start us, length us, event | category | flops | bytes accessed | tf_op | source)
XLA Modules:
  0.0 196.7 jit_solution(2688861441149911159)
XLA Ops:
  0.0 1.0 convert_reduce_fusion
  1.0 0.8 dynamic_slice.6
  1.8 0.7 select_reduce_fusion.1
  2.6 0.2 and_select_fusion
  2.7 0.8 fusion.3
  3.6 0.7 select_convert_fusion.qaug_ref
  4.3 0.3 multiply_cosine_fusion
  4.7 0.7 pad_maximum_fusion
  5.4 0.8 fusion.kaug_ref
  6.1 187.8 %shard_map.37 = bf16[384,2304]{1,0:T(8,128)(2,1)} custom-call(bf16[384,6912]{1,0:T(8,128)(2,1)} %x_ref.1, f32[4,24,384]{2,1,0:T(8,128)} %bitcast.1, bf16[12,32,384]{2,1,0:T(8,128)(2,1)} %fusion.kaug_ref, bf16[4,32,384]{2,1,0:T(8,128)(2,1)} %select_convert_fusion.qaug_ref), custom_call_target="tpu_custom_call" | custom-call | flops 10871635968 | bytes 7077888 | tf_op jit(solution)/shard_map/pallas_call | solution.py:270
  193.9 2.8 %copy.5 = bf16[384,2304]{1,0:T(8,128)(2,1)} copy(bf16[384,2304]{1,0:T(8,128)(2,1)} %shard_map.37) | data formatting | bytes 3538944
  (7 shorter events, 0.1 us)

commit v2 on v1

--- a/solution.py
+++ b/solution.py
@@ -22,13 +22,13 @@
 
 
 def kernel(
-    group, chunks, seqs, x_ref, turns_ref, kaug_ref, qaug_ref, out_ref,
-    send, held, keys, blended, back,
+    group, chunks, seqs, count, x_ref, turns_ref, seg_ref, out_ref,
+    send, held, keys, values, queries, blended, back,
     in_send, in_recv, in_own, halo_send, halo_recv, back_send, back_recv, back_own,
 ):
     tok = x_ref.shape[0]
     span = group * HEAD
-    aug = kaug_ref.shape[1]
+    aug = queries.shape[0] - HEAD
     seq = lax.axis_index("seq")
     me = lax.axis_index("head")
     has_left = seq > 0
@@ -53,13 +53,16 @@
         barrier, group - 1 + has_left.astype(jnp.int32) + has_right.astype(jnp.int32)
     )
 
-    def in_copy(j, d):
+    parts = ((0, 2), (2, 1))
+
+    def in_copy(j, d, which):
         dest = lax.rem(me + d, group)
+        first, size = parts[which]
         return pltpu.make_async_remote_copy(
-            src_ref=send.at[j, dest],
-            dst_ref=held.at[j, group + me],
-            send_sem=in_send.at[j, d - 1],
-            recv_sem=in_recv.at[j, d - 1],
+            src_ref=send.at[j, dest, pl.ds(first, size)],
+            dst_ref=held.at[j, group + me, pl.ds(first, size)],
+            send_sem=in_send.at[j, d - 1, which],
+            recv_sem=in_recv.at[j, d - 1, which],
             device_id={"head": dest},
             device_id_type=MESH,
         )
@@ -70,8 +73,8 @@
     def halo_copy(j, side):
         slot = 0 if side == 0 else 2 * group
         return pltpu.make_async_remote_copy(
-            src_ref=held.at[j, pl.ds(group, group), pl.ds(1, 2)],
-            dst_ref=held.at[j, pl.ds(slot, group), pl.ds(1, 2)],
+            src_ref=held.at[j, pl.ds(group, group), pl.ds(0, 2)],
+            dst_ref=held.at[j, pl.ds(slot, group), pl.ds(0, 2)],
             send_sem=halo_send.at[j, side],
             recv_sem=halo_recv.at[j, side],
             device_id={"seq": seq + 1 if side == 0 else seq - 1},
@@ -92,8 +95,8 @@
     def back_own_copy(j):
         return pltpu.make_async_copy(blended.at[j, me], back.at[j, me], back_own.at[j])
 
-    def issue(j):
-        for part in range(3):
+    def prepare(j):
+        for place, part in enumerate((1, 2, 0)):
             first = pl.multiple_of(part * D + j * span, 128)
             cols = transposed(x_ref[:, pl.ds(first, span)])
             for z in range(group):
@@ -106,16 +109,21 @@
                         high = vals[(2 * half + 1) * QUARTER:(2 * half + 2) * QUARTER]
                         pieces += [low * cosine - high * sine, low * sine + high * cosine]
                     vals = jnp.concatenate(pieces, axis=0)
-                send[j, z, part] = vals.astype(jnp.bfloat16)
-        for d in range(1, group):
-            in_copy(j, d).start()
-        own_copy(j).start()
-
-    def arrive(j):
-        own_copy(j).wait()
-        for d in range(1, group):
-            in_copy(j, d).wait_recv()
-
+                send[j, z, place] = vals.astype(jnp.bfloat16)
+
+    def issue(j, which):
+        for d in range(1, group):
+            in_copy(j, d, which).start()
+        if which == 0:
+            own_copy(j).start()
+
+    def arrive(j, which):
+        if which == 0:
+            own_copy(j).wait()
+        for d in range(1, group):
+            in_copy(j, d, which).wait_recv()
+
+    def halo_start(j):
         @pl.when(has_right)
         def _():
             halo_copy(j, 0).start()
@@ -143,64 +151,92 @@
             for z in range(group):
                 held[j, 2 * group + z] = jnp.zeros((3, HEAD, tok), jnp.bfloat16)
 
-    window = 2 * group + 1
-    several = 3 if window % 3 == 0 else 1
-
-    def attend(j):
-        def lay(slot, carry):
-            joined = jnp.concatenate([held[j, slot, 1], kaug_ref[slot]], axis=0)
-            keys[slot] = transposed(joined).astype(jnp.bfloat16)
-            return carry
-
-        lax.fori_loop(0, 3 * group, lay, 0)
-        ones = jnp.ones((ONES, tok), jnp.bfloat16)
-
-        def query_block(i, carry):
-            q = jnp.concatenate([held[j, group + i, 0], qaug_ref[i]], axis=0)
-
-            def key_blocks(step, state):
-                top, acc = state
-                scores = []
-                for b in range(several):
-                    scores.append(
-                        jnp.dot(keys[i + step * several + b], q, preferred_element_type=jnp.float32)
-                    )
-                new_top = top
-                for s in scores:
-                    new_top = jnp.maximum(new_top, jnp.max(s, axis=0, keepdims=True))
-                acc = acc * jnp.exp2((top - new_top) * scale)
-                for b, s in enumerate(scores):
-                    weights = jnp.exp2((s - new_top) * scale).astype(jnp.bfloat16)
-                    v = jnp.concatenate([held[j, i + step * several + b, 2], ones], axis=0)
-                    acc = acc + jnp.dot(v, weights, preferred_element_type=jnp.float32)
-                return new_top, acc
-
-            top = jnp.full((1, tok), -1e30, jnp.float32)
-            acc = jnp.zeros((HEAD + ONES, tok), jnp.float32)
-            top, acc = lax.fori_loop(0, window // several, key_blocks, (top, acc))
-            blended[j, i] = (acc[:HEAD] / acc[HEAD:HEAD + 1]).astype(jnp.bfloat16)
-            return carry
-
-        lax.fori_loop(0, group, query_block, 0)
+    def back_start(j):
         for d in range(1, group):
             back_copy(j, d).start()
         back_own_copy(j).start()
 
-    issue(0)
+    wide = 2 * tok
+    lane = lax.broadcasted_iota(jnp.int32, (aug, tok), 0)
+
+    def attend(j):
+        for slot in range(3 * group):
+            hot = jnp.where(seg_ref[slot] == lane, 1.0, 0.0)
+            joined = jnp.concatenate([held[j, slot, 0].astype(jnp.float32), hot], axis=0)
+            keys[pl.ds(slot * tok, tok)] = transposed(joined).astype(jnp.bfloat16)
+            values[:HEAD, pl.ds(slot * tok, tok)] = held[j, slot, 1]
+        for z in range(group):
+            queries[:HEAD, pl.ds(z * tok, tok)] = held[j, group + z, 2]
+
+        def query_block(i, carry):
+            base = i * wide
+            q = queries[:, pl.ds(pl.multiple_of(base, 128), wide)]
+
+            def key_block(step, state):
+                top, acc = state
+                start = pl.multiple_of(base + step * wide, 128)
+                s = jnp.dot(keys[pl.ds(start, wide)], q, preferred_element_type=jnp.float32)
+                new_top = jnp.maximum(top, jnp.max(s, axis=0, keepdims=True))
+                weights = jnp.exp2((s - new_top) * scale).astype(jnp.bfloat16)
+                acc = acc * jnp.exp2((top - new_top) * scale) + jnp.dot(
+                    values[:, pl.ds(start, wide)], weights, preferred_element_type=jnp.float32
+                )
+                return new_top, acc
+
+            top = jnp.full((1, wide), -1e30, jnp.float32)
+            acc = jnp.zeros((HEAD + ONES, wide), jnp.float32)
+            top, acc = lax.fori_loop(0, group + 1, key_block, (top, acc))
+            mean = (acc[:HEAD] / acc[HEAD:HEAD + 1]).astype(jnp.bfloat16)
+            blended[j, 2 * i] = mean[:, :tok]
+            blended[j, 2 * i + 1] = mean[:, tok:]
+            return carry
+
+        lax.fori_loop(0, group // 2, query_block, 0)
+
+    prepare(0)
+    issue(0, 0)
+    issue(0, 1)
+    prepare(1)
+    values[HEAD:] = jnp.ones((ONES, values.shape[1]), jnp.bfloat16)
+    for z in range(group):
+        same = (seg_ref[group + z] == lane) | (lane > count)
+        queries[HEAD:, pl.ds(z * tok, tok)] = jnp.where(same, 0.0, APART).astype(jnp.bfloat16)
 
     def step(t, carry):
+        @pl.when(t < chunks)
+        def _():
+            arrive(t, 0)
+            halo_start(t)
+
         @pl.when(t + 1 < chunks)
         def _():
-            issue(t + 1)
+            issue(t + 1, 0)
 
         @pl.when(t < chunks)
         def _():
-            arrive(t)
+            arrive(t, 1)
+
+        @pl.when(t + 1 < chunks)
+        def _():
+            issue(t + 1, 1)
+
+        @pl.when(t + 2 < chunks)
+        def _():
+            prepare(t + 2)
+
+        @pl.when(t == chunks - 1)
+        def _():
+            for j in range(chunks - 2):
+                back_start(j)
 
         @pl.when(t >= 1)
         def _():
             halo_arrive(t - 1)
             attend(t - 1)
+
+        @pl.when(t >= chunks - 1)
+        def _():
+            back_start(t - 1)
 
         return carry
 
@@ -215,7 +251,8 @@
             jnp.bfloat16
         )
         for d in range(1, group):
-            in_copy(j, d).wait_send()
+            in_copy(j, d, 0).wait_send()
+            in_copy(j, d, 1).wait_send()
             back_copy(j, d).wait_send()
 
         @pl.when(has_right)
@@ -259,27 +296,25 @@
     none = jnp.full((shard,), count, jnp.int32)
     padded = jnp.concatenate([none, segment_ids, none])
     key_seg = lax.dynamic_slice_in_dim(padded, seq * shard, 3 * shard, 0)
-    lanes = jnp.arange(aug, dtype=jnp.int32)[None, :, None]
     key_seg = key_seg.reshape(3 * group, 1, tok)
-    kaug = (key_seg == lanes).astype(jnp.bfloat16)
-    query_seg = key_seg[group:2 * group]
-    qaug = jnp.where((query_seg == lanes) | (lanes > count), 0.0, APART).astype(jnp.bfloat16)
 
     vmem = pl.BlockSpec(memory_space=pltpu.VMEM)
     dma = pltpu.SemaphoreType.DMA
     return pl.pallas_call(
-        functools.partial(kernel, group, chunks, seqs),
+        functools.partial(kernel, group, chunks, seqs, count),
         out_shape=jax.ShapeDtypeStruct((tok, D), jnp.bfloat16),
-        in_specs=[vmem] * 4,
+        in_specs=[vmem] * 3,
         out_specs=vmem,
         scratch_shapes=[
             pltpu.VMEM((chunks, group, 3, HEAD, tok), jnp.bfloat16),
             pltpu.VMEM((chunks, 3 * group, 3, HEAD, tok), jnp.bfloat16),
-            pltpu.VMEM((3 * group, tok, HEAD + aug), jnp.bfloat16),
+            pltpu.VMEM((3 * shard, HEAD + aug), jnp.bfloat16),
+            pltpu.VMEM((HEAD + ONES, 3 * shard), jnp.bfloat16),
+            pltpu.VMEM((HEAD + aug, shard), jnp.bfloat16),
             pltpu.VMEM((chunks, group, HEAD, tok), jnp.bfloat16),
             pltpu.VMEM((chunks, group, HEAD, tok), jnp.bfloat16),
-            dma((chunks, group - 1)),
-            dma((chunks, group - 1)),
+            dma((chunks, group - 1, 2)),
+            dma((chunks, group - 1, 2)),
             dma((chunks,)),
             dma((chunks, 2)),
             dma((chunks, 2)),
@@ -293,7 +328,7 @@
         cost_estimate=pl.CostEstimate(
             flops=4 * shard * shard * 2 * D // group, bytes_accessed=tok * D * 8, transcendentals=0
         ),
-    )(projected, turns, kaug, qaug)
+    )(projected, turns, key_seg)
 
 
 def solution(mesh):

time: 197 us -> 175 us (0.89)
  Pallas kernels: 188 us -> 167 us
    pallas_call x1, Pallas kernels: 188 us -> 167 us  [body(): pl.pallas_call(functools.partial(kernel, group, chunks, seqs, count), out...]
where the time goes in v2:
time: 175 us
  Pallas kernels  167 us (95%)
  local copies, waits for them, and re-layouts  4.2 us (2%)
  other arithmetic  3.77 us (2%)
    pallas_call x1, Pallas kernels, body(): pl.pallas_call(functools.partial(kernel, group, chunks, seqs, count), out...  167 us

profile of v2, /device:TPU:0, one launch (start us, length us, event | category | flops | bytes accessed | tf_op | source)
XLA Modules:
  0.0 174.7 jit_solution(404032507308909445)
XLA Ops:
  0.0 1.0 convert_reduce_fusion
  1.0 0.8 dynamic_slice.6
  1.8 0.7 select_reduce_fusion.1
  2.5 0.2 and_select_fusion
  2.7 0.8 fusion.1
  3.6 0.6 reshape.107.seg_ref
  4.2 0.3 multiply_cosine_fusion
  4.5 0.7 pad_maximum_fusion
  5.2 166.7 %shard_map.37 = bf16[384,2304]{1,0:T(8,128)(2,1)} custom-call(bf16[384,6912]{1,0:T(8,128)(2,1)} %x_ref.1, f32[4,24,384]{2,1,0:T(8,128)} %bitcast.1, s32[12,1,384]{2,1,0:T(1,128)} %reshape.107.seg_ref), custom_call_target="tpu_custom_call" | custom-call | flops 10871635968 | bytes 7077888 | tf_op jit(solution)/shard_map/pallas_call | solution.py:303
  172.0 2.8 %copy.5 = bf16[384,2304]{1,0:T(8,128)(2,1)} copy(bf16[384,2304]{1,0:T(8,128)(2,1)} %shard_map.37) | data formatting | bytes 3538944
  (3 shorter events, 0.0 us)

commit v3 on v2

--- a/solution.py
+++ b/solution.py
@@ -22,11 +22,12 @@
 
 
 def kernel(
-    group, chunks, seqs, count, x_ref, turns_ref, seg_ref, out_ref,
-    send, held, keys, values, queries, blended, back,
-    in_send, in_recv, in_own, halo_send, halo_recv, back_send, back_recv, back_own,
+    group, chunks, seqs, count, x_ref, freq_ref, widths_ref, seg_ref, out_ref,
+    x_held, turns, key_seg, send, held, keys, values, queries, blended, back,
+    x_sem, in_send, in_recv, in_own, halo_send, halo_recv, back_send, back_recv, back_own,
 ):
     tok = x_ref.shape[0]
+    blocks = seqs * group
     span = group * HEAD
     aug = queries.shape[0] - HEAD
     seq = lax.axis_index("seq")
@@ -35,6 +36,18 @@
     has_right = seq < seqs - 1
     scale = math.log2(math.e) / math.sqrt(HEAD)
 
+    columns = (2 * D, D, 0)
+
+    def x_copy(j, part):
+        first = pl.multiple_of(columns[part] + j * span, 128)
+        return pltpu.make_async_copy(
+            x_ref.at[:, pl.ds(first, span)], x_held.at[j, part], x_sem.at[j, part]
+        )
+
+    for j in range(chunks):
+        for part in range(3):
+            x_copy(j, part).start()
+
     barrier = pltpu.get_barrier_semaphore()
     for d in range(1, group):
         pl.semaphore_signal(
@@ -53,22 +66,21 @@
         barrier, group - 1 + has_left.astype(jnp.int32) + has_right.astype(jnp.int32)
     )
 
-    parts = ((0, 2), (2, 1))
-
-    def in_copy(j, d, which):
+    def in_copy(j, d, part):
         dest = lax.rem(me + d, group)
-        first, size = parts[which]
         return pltpu.make_async_remote_copy(
-            src_ref=send.at[j, dest, pl.ds(first, size)],
-            dst_ref=held.at[j, group + me, pl.ds(first, size)],
-            send_sem=in_send.at[j, d - 1, which],
-            recv_sem=in_recv.at[j, d - 1, which],
+            src_ref=send.at[j, dest, part],
+            dst_ref=held.at[j, group + me, part],
+            send_sem=in_send.at[j, d - 1, part],
+            recv_sem=in_recv.at[j, d - 1, part],
             device_id={"head": dest},
             device_id_type=MESH,
         )
 
-    def own_copy(j):
-        return pltpu.make_async_copy(send.at[j, me], held.at[j, group + me], in_own.at[j])
+    def own_copy(j, part):
+        return pltpu.make_async_copy(
+            send.at[j, me, part], held.at[j, group + me, part], in_own.at[j, part]
+        )
 
     def halo_copy(j, side):
         slot = 0 if side == 0 else 2 * group
@@ -95,33 +107,56 @@
     def back_own_copy(j):
         return pltpu.make_async_copy(blended.at[j, me], back.at[j, me], back_own.at[j])
 
-    def prepare(j):
-        for place, part in enumerate((1, 2, 0)):
-            first = pl.multiple_of(part * D + j * span, 128)
-            cols = transposed(x_ref[:, pl.ds(first, span)])
-            for z in range(group):
-                vals = cols[z * HEAD:(z + 1) * HEAD]
-                if part < 2:
-                    pieces = []
-                    for half in range(2):
-                        cosine, sine = turns_ref[2 * half], turns_ref[2 * half + 1]
-                        low = vals[2 * half * QUARTER:(2 * half + 1) * QUARTER]
-                        high = vals[(2 * half + 1) * QUARTER:(2 * half + 2) * QUARTER]
-                        pieces += [low * cosine - high * sine, low * sine + high * cosine]
-                    vals = jnp.concatenate(pieces, axis=0)
-                send[j, z, place] = vals.astype(jnp.bfloat16)
-
-    def issue(j, which):
-        for d in range(1, group):
-            in_copy(j, d, which).start()
-        if which == 0:
-            own_copy(j).start()
-
-    def arrive(j, which):
-        if which == 0:
-            own_copy(j).wait()
-        for d in range(1, group):
-            in_copy(j, d, which).wait_recv()
+    def prepare(j, part):
+        x_copy(j, part).wait()
+        cols = transposed(x_held[j, part])
+        for z in range(group):
+            vals = cols[z * HEAD:(z + 1) * HEAD]
+            if part > 0:
+                pieces = []
+                for half in range(2):
+                    cosine, sine = turns[2 * half], turns[2 * half + 1]
+                    low = vals[2 * half * QUARTER:(2 * half + 1) * QUARTER]
+                    high = vals[(2 * half + 1) * QUARTER:(2 * half + 2) * QUARTER]
+                    pieces += [low * cosine - high * sine, low * sine + high * cosine]
+                vals = jnp.concatenate(pieces, axis=0)
+            send[j, z, part] = vals.astype(jnp.bfloat16)
+
+    def issue(j, part):
+        for d in range(1, group):
+            in_copy(j, d, part).start()
+        own_copy(j, part).start()
+
+    def arrive(j, part):
+        own_copy(j, part).wait()
+        for d in range(1, group):
+            in_copy(j, d, part).wait_recv()
+
+    def lay_out():
+        block = seq * group + me
+        own = seg_ref[pl.ds(block, 1), :]
+        everything = seg_ref[...]
+        start = jnp.zeros((1, tok), jnp.int32)
+        width = jnp.zeros((1, tok), jnp.int32)
+        for sample in range(count):
+            lower = jnp.sum(
+                jnp.sum((everything < sample).astype(jnp.int32), axis=0, keepdims=True),
+                axis=1, keepdims=True,
+            )
+            start = jnp.where(own == sample, lower, start)
+            width = jnp.where(own == sample, widths_ref[sample], width)
+        offset = block * tok + lax.broadcasted_iota(jnp.int32, (1, tok), 1) - start
+        row = jnp.floor((offset.astype(jnp.float32) + 0.5) / width.astype(jnp.float32))
+        col = offset.astype(jnp.float32) - row * width.astype(jnp.float32)
+        for half, place in enumerate((row, col)):
+            angles = freq_ref[...] * place
+            turns[2 * half] = jnp.cos(angles)
+            turns[2 * half + 1] = jnp.sin(angles)
+        for slot in range(3 * group):
+            number = (seq - 1) * group + slot
+            ids = seg_ref[pl.ds(jnp.clip(number, 0, blocks - 1), 1), :]
+            outside = jnp.logical_or(number < 0, number >= blocks).astype(jnp.int32)
+            key_seg[slot] = ids * (1 - outside) + count * outside
 
     def halo_start(j):
         @pl.when(has_right)
@@ -159,15 +194,16 @@
     wide = 2 * tok
     lane = lax.broadcasted_iota(jnp.int32, (aug, tok), 0)
 
-    def attend(j):
+    def gather(j):
         for slot in range(3 * group):
-            hot = jnp.where(seg_ref[slot] == lane, 1.0, 0.0)
-            joined = jnp.concatenate([held[j, slot, 0].astype(jnp.float32), hot], axis=0)
+            hot = jnp.where(key_seg[slot] == lane, 1.0, 0.0)
+            joined = jnp.concatenate([held[j, slot, 1].astype(jnp.float32), hot], axis=0)
             keys[pl.ds(slot * tok, tok)] = transposed(joined).astype(jnp.bfloat16)
-            values[:HEAD, pl.ds(slot * tok, tok)] = held[j, slot, 1]
+            values[:HEAD, pl.ds(slot * tok, tok)] = held[j, slot, 0]
         for z in range(group):
             queries[:HEAD, pl.ds(z * tok, tok)] = held[j, group + z, 2]
 
+    def attend(j, first, last):
         def query_block(i, carry):
             base = i * wide
             q = queries[:, pl.ds(pl.multiple_of(base, 128), wide)]
@@ -191,52 +227,66 @@
             blended[j, 2 * i + 1] = mean[:, tok:]
             return carry
 
-        lax.fori_loop(0, group // 2, query_block, 0)
-
-    prepare(0)
+        lax.fori_loop(first, last, query_block, 0)
+
+    prepare(0, 0)
     issue(0, 0)
-    issue(0, 1)
-    prepare(1)
+    lay_out()
+    for part in (1, 2):
+        prepare(0, part)
+        issue(0, part)
+    for part in range(3):
+        prepare(1, part)
     values[HEAD:] = jnp.ones((ONES, values.shape[1]), jnp.bfloat16)
     for z in range(group):
-        same = (seg_ref[group + z] == lane) | (lane > count)
+        same = (key_seg[group + z] == lane) | (lane > count)
         queries[HEAD:, pl.ds(z * tok, tok)] = jnp.where(same, 0.0, APART).astype(jnp.bfloat16)
 
+    pairs = group // 2
+
     def step(t, carry):
+        @pl.when(t >= 1)
+        def _():
+            halo_arrive(t - 1)
+            gather(t - 1)
+            attend(t - 1, 0, pairs // 2)
+
         @pl.when(t < chunks)
         def _():
             arrive(t, 0)
+            arrive(t, 1)
             halo_start(t)
 
         @pl.when(t + 1 < chunks)
         def _():
             issue(t + 1, 0)
+            issue(t + 1, 1)
+
+        @pl.when(t >= 1)
+        def _():
+            attend(t - 1, pairs // 2, pairs)
 
         @pl.when(t < chunks)
         def _():
-            arrive(t, 1)
+            arrive(t, 2)
 
         @pl.when(t + 1 < chunks)
         def _():
-            issue(t + 1, 1)
-
-        @pl.when(t + 2 < chunks)
-        def _():
-            prepare(t + 2)
+            issue(t + 1, 2)
 
         @pl.when(t == chunks - 1)
         def _():
             for j in range(chunks - 2):
                 back_start(j)
 
-        @pl.when(t >= 1)
-        def _():
-            halo_arrive(t - 1)
-            attend(t - 1)
-
         @pl.when(t >= chunks - 1)
         def _():
             back_start(t - 1)
+
+        @pl.when(t + 2 < chunks)
+        def _():
+            for part in range(3):
+                prepare(t + 2, part)
 
         return carry
 
@@ -251,8 +301,8 @@
             jnp.bfloat16
         )
         for d in range(1, group):
-            in_copy(j, d, 0).wait_send()
-            in_copy(j, d, 1).wait_send()
+            for part in range(3):
+                in_copy(j, d, part).wait_send()
             back_copy(j, d).wait_send()
 
         @pl.when(has_right)
@@ -274,38 +324,23 @@
     seqs = lax.axis_size("seq")
     chunks = HEADS // group
     shard = tok * group
-    seq = lax.axis_index("seq")
-    first = (seq * group + lax.axis_index("head")) * tok
-    ids = jnp.arange(widths.shape[0], dtype=jnp.int32)
-
-    starts = jnp.sum((segment_ids[None, :] < ids[:, None]).astype(jnp.int32), axis=1)
-    own = lax.dynamic_slice_in_dim(segment_ids, first, tok, 0)
-    mine = own[None, :] == ids[:, None]
-    own_start = jnp.sum(jnp.where(mine, starts[:, None], 0), axis=0)
-    width = jnp.sum(jnp.where(mine, widths[:, None], 0), axis=0)
-    offset = first + jnp.arange(tok, dtype=jnp.int32) - own_start
-    row_pos = offset // width
-    col_pos = offset - row_pos * width
-    frequency = 10000.0 ** (-jnp.arange(QUARTER, dtype=jnp.float32) / QUARTER)
-    places = jnp.stack([row_pos, col_pos]).astype(jnp.float32)
-    angles = places[:, None, :] * frequency[None, :, None]
-    turns = jnp.stack([jnp.cos(angles), jnp.sin(angles)], axis=1).reshape(4, QUARTER, tok)
-
     count = widths.shape[0]
     aug = -(-(HEAD + count + 1) // 128) * 128 - HEAD
-    none = jnp.full((shard,), count, jnp.int32)
-    padded = jnp.concatenate([none, segment_ids, none])
-    key_seg = lax.dynamic_slice_in_dim(padded, seq * shard, 3 * shard, 0)
-    key_seg = key_seg.reshape(3 * group, 1, tok)
+    frequency = 10000.0 ** (-jnp.arange(QUARTER, dtype=jnp.float32) / QUARTER)
 
     vmem = pl.BlockSpec(memory_space=pltpu.VMEM)
     dma = pltpu.SemaphoreType.DMA
     return pl.pallas_call(
         functools.partial(kernel, group, chunks, seqs, count),
         out_shape=jax.ShapeDtypeStruct((tok, D), jnp.bfloat16),
-        in_specs=[vmem] * 3,
+        in_specs=[
+            pl.BlockSpec(memory_space=pl.ANY), vmem, pl.BlockSpec(memory_space=pltpu.SMEM), vmem
+        ],
         out_specs=vmem,
         scratch_shapes=[
+            pltpu.VMEM((chunks, 3, tok, group * HEAD), jnp.bfloat16),
+            pltpu.VMEM((4, QUARTER, tok), jnp.float32),
+            pltpu.VMEM((3 * group, 1, tok), jnp.int32),
             pltpu.VMEM((chunks, group, 3, HEAD, tok), jnp.bfloat16),
             pltpu.VMEM((chunks, 3 * group, 3, HEAD, tok), jnp.bfloat16),
             pltpu.VMEM((3 * shard, HEAD + aug), jnp.bfloat16),
@@ -313,9 +348,10 @@
             pltpu.VMEM((HEAD + aug, shard), jnp.bfloat16),
             pltpu.VMEM((chunks, group, HEAD, tok), jnp.bfloat16),
             pltpu.VMEM((chunks, group, HEAD, tok), jnp.bfloat16),
-            dma((chunks, group - 1, 2)),
-            dma((chunks, group - 1, 2)),
-            dma((chunks,)),
+            dma((chunks, 3)),
+            dma((chunks, group - 1, 3)),
+            dma((chunks, group - 1, 3)),
+            dma((chunks, 3)),
             dma((chunks, 2)),
             dma((chunks, 2)),
             dma((chunks, group - 1)),
@@ -328,7 +364,7 @@
         cost_estimate=pl.CostEstimate(
             flops=4 * shard * shard * 2 * D // group, bytes_accessed=tok * D * 8, transcendentals=0
         ),
-    )(projected, turns, key_seg)
+    )(projected, frequency[:, None], widths, segment_ids.reshape(seqs * group, tok))
 
 
 def solution(mesh):

time: 175 us -> 170 us (0.971); the launches traced: 175 us -> 167 us
  Pallas kernels: 167 us -> 162 us
  other arithmetic: 3.77 us -> 0.61 us
    pallas_call x1, Pallas kernels: 167 us -> 162 us  [body(): pl.pallas_call(functools.partial(kernel, group, chunks, seqs, count), out...]
    reduce_sum x2 -> x0, other arithmetic: 1.75 us -> none  [the longest x1 1.01 us: body(): jnp.sum((segment_ids[None, :] < ids[:, None]).astype(jnp.int32), axis=1)]
where the time goes in v3:
time: 170 us; the launch traced here: 167 us
  Pallas kernels  162 us (95%)
  local copies, waits for them, and re-layouts  4.23 us (2%)
    pallas_call x1, Pallas kernels, body(): pl.pallas_call(functools.partial(kernel, group, chunks, seqs, count), out...  162 us

profile of v3, /device:TPU:0, one launch (start us, length us, event | category | flops | bytes accessed | tf_op | source)
XLA Modules:
  0.0 166.9 jit_solution(3087701537010808571)
XLA Ops:
  0.0 0.6 multiply_power_fusion.freq_ref
  0.6 1.4 reshape.16.seg_ref
  2.0 162.1 %shard_map.37 = bf16[384,2304]{1,0:T(8,128)(2,1)} custom-call(bf16[384,6912]{1,0:T(8,128)(2,1)} %x_ref.1, f32[24,1]{1,0:T(8,128)} %multiply_power_fusion.freq_ref, s32[16]{0:T(128)} %widths_ref.1, s32[32,384]{1,0:T(8,128)} %reshape.16.seg_ref), custom_call_target="tpu_custom_call" | custom-call | flops 10871635968 | bytes 7077888 | tf_op jit(solution)/shard_map/pallas_call | solution.py:333
  164.1 2.8 %copy.5 = bf16[384,2304]{1,0:T(8,128)(2,1)} copy(bf16[384,2304]{1,0:T(8,128)(2,1)} %shard_map.37) | data formatting | bytes 3538944

commit v4 on v3

--- a/solution.py
+++ b/solution.py
@@ -3,6 +3,7 @@
 
 import jax
 import jax.numpy as jnp
+import numpy as np
 from jax import lax
 from jax.experimental import pallas as pl
 from jax.experimental.pallas import tpu as pltpu
@@ -18,7 +19,7 @@
 
 
 def transposed(block):
-    return jnp.transpose(block.astype(jnp.float32), (1, 0))
+    return jnp.transpose(block, (1, 0))
 
 
 def kernel(
@@ -113,6 +114,7 @@
         for z in range(group):
             vals = cols[z * HEAD:(z + 1) * HEAD]
             if part > 0:
+                vals = vals.astype(jnp.float32)
                 pieces = []
                 for half in range(2):
                     cosine, sine = turns[2 * half], turns[2 * half + 1]
@@ -132,9 +134,15 @@
         for d in range(1, group):
             in_copy(j, d, part).wait_recv()
 
+    rows = tok // seg_ref.shape[1]
+
+    def ids_of(block):
+        pieces = [seg_ref[pl.ds(block * rows + r, 1), :] for r in range(rows)]
+        return jnp.concatenate(pieces, axis=1)
+
     def lay_out():
         block = seq * group + me
-        own = seg_ref[pl.ds(block, 1), :]
+        own = ids_of(block)
         everything = seg_ref[...]
         start = jnp.zeros((1, tok), jnp.int32)
         width = jnp.zeros((1, tok), jnp.int32)
@@ -154,7 +162,7 @@
             turns[2 * half + 1] = jnp.sin(angles)
         for slot in range(3 * group):
             number = (seq - 1) * group + slot
-            ids = seg_ref[pl.ds(jnp.clip(number, 0, blocks - 1), 1), :]
+            ids = ids_of(jnp.clip(number, 0, blocks - 1))
             outside = jnp.logical_or(number < 0, number >= blocks).astype(jnp.int32)
             key_seg[slot] = ids * (1 - outside) + count * outside
 
@@ -186,19 +194,26 @@
             for z in range(group):
                 held[j, 2 * group + z] = jnp.zeros((3, HEAD, tok), jnp.bfloat16)
 
-    def back_start(j):
-        for d in range(1, group):
-            back_copy(j, d).start()
-        back_own_copy(j).start()
+    def back_start(j, first=0, last=group):
+        for d in range(1, group):
+            dest = lax.rem(me + d, group)
+
+            @pl.when(jnp.logical_and(dest >= first, dest < last))
+            def _():
+                back_copy(j, d).start()
+
+        @pl.when(jnp.logical_and(me >= first, me < last))
+        def _():
+            back_own_copy(j).start()
 
     wide = 2 * tok
     lane = lax.broadcasted_iota(jnp.int32, (aug, tok), 0)
 
     def gather(j):
         for slot in range(3 * group):
-            hot = jnp.where(key_seg[slot] == lane, 1.0, 0.0)
-            joined = jnp.concatenate([held[j, slot, 1].astype(jnp.float32), hot], axis=0)
-            keys[pl.ds(slot * tok, tok)] = transposed(joined).astype(jnp.bfloat16)
+            hot = jnp.where(key_seg[slot] == lane, 1.0, 0.0).astype(jnp.bfloat16)
+            joined = jnp.concatenate([held[j, slot, 1], hot], axis=0)
+            keys[pl.ds(slot * tok, tok)] = transposed(joined)
             values[:HEAD, pl.ds(slot * tok, tok)] = held[j, slot, 0]
         for z in range(group):
             queries[:HEAD, pl.ds(z * tok, tok)] = held[j, group + z, 2]
@@ -251,6 +266,10 @@
             gather(t - 1)
             attend(t - 1, 0, pairs // 2)
 
+        @pl.when(t == chunks)
+        def _():
+            back_start(t - 1, 0, pairs // 2 * 2)
+
         @pl.when(t < chunks)
         def _():
             arrive(t, 0)
@@ -259,29 +278,29 @@
 
         @pl.when(t + 1 < chunks)
         def _():
-            issue(t + 1, 0)
-            issue(t + 1, 1)
-
-        @pl.when(t >= 1)
-        def _():
-            attend(t - 1, pairs // 2, pairs)
-
-        @pl.when(t < chunks)
-        def _():
-            arrive(t, 2)
-
-        @pl.when(t + 1 < chunks)
-        def _():
-            issue(t + 1, 2)
+            for part in range(3):
+                issue(t + 1, part)
 
         @pl.when(t == chunks - 1)
         def _():
             for j in range(chunks - 2):
                 back_start(j)
 
-        @pl.when(t >= chunks - 1)
+        @pl.when(t >= 1)
+        def _():
+            attend(t - 1, pairs // 2, pairs)
+
+        @pl.when(t < chunks)
+        def _():
+            arrive(t, 2)
+
+        @pl.when(t == chunks - 1)
         def _():
             back_start(t - 1)
+
+        @pl.when(t == chunks)
+        def _():
+            back_start(t - 1, pairs // 2 * 2, group)
 
         @pl.when(t + 2 < chunks)
         def _():
@@ -297,9 +316,7 @@
         for d in range(1, group):
             back_copy(j, d).wait_recv()
         rows = jnp.concatenate([back[j, z] for z in range(group)], axis=0)
-        out_ref[:, pl.ds(pl.multiple_of(j * span, 128), span)] = transposed(rows).astype(
-            jnp.bfloat16
-        )
+        out_ref[:, pl.ds(pl.multiple_of(j * span, 128), span)] = transposed(rows)
         for d in range(1, group):
             for part in range(3):
                 in_copy(j, d, part).wait_send()
@@ -326,7 +343,8 @@
     shard = tok * group
     count = widths.shape[0]
     aug = -(-(HEAD + count + 1) // 128) * 128 - HEAD
-    frequency = 10000.0 ** (-jnp.arange(QUARTER, dtype=jnp.float32) / QUARTER)
+    frequency = 10000.0 ** (-np.arange(QUARTER, dtype=np.float64) / QUARTER)
+    frequency = jnp.asarray(frequency.astype(np.float32))
 
     vmem = pl.BlockSpec(memory_space=pltpu.VMEM)
     dma = pltpu.SemaphoreType.DMA
@@ -364,7 +382,7 @@
         cost_estimate=pl.CostEstimate(
             flops=4 * shard * shard * 2 * D // group, bytes_accessed=tok * D * 8, transcendentals=0
         ),
-    )(projected, frequency[:, None], widths, segment_ids.reshape(seqs * group, tok))
+    )(projected, frequency[:, None], widths, segment_ids.reshape(-1, 128 if tok % 128 == 0 else tok))
 
 
 def solution(mesh):

time: 170 us -> 165 us (0.971); the launches traced: 167 us -> 164 us
  no operation moved by 1% of the time
where the time goes in v4:
time: 165 us; the launch traced here: 164 us
  Pallas kernels  162 us (98%)
  local copies, waits for them, and re-layouts  2.8 us (2%)
    pallas_call x1, Pallas kernels, body(): pl.pallas_call(functools.partial(kernel, group, chunks, seqs, count), out...  162 us

profile of v4, /device:TPU:0, one launch (start us, length us, event | category | flops | bytes accessed | tf_op | source)
XLA Modules:
  0.0 164.3 jit_solution(8577323399774346023)
XLA Ops:
  0.0 161.5 %shard_map.46 = bf16[384,2304]{1,0:T(8,128)(2,1)} custom-call(bf16[384,6912]{1,0:T(8,128)(2,1)} %x_ref.1, f32[24,1]{1,0:T(8,128)} %constant.3.freq_ref, s32[16]{0:T(128)} %widths_ref.1, s32[96,128]{1,0:T(8,128)} %bitcast.1), custom_call_target="tpu_custom_call" | custom-call | flops 10871635968 | bytes 7077888 | tf_op jit(solution)/shard_map/pallas_call | solution.py:351
  161.5 2.8 %copy.6 = bf16[384,2304]{1,0:T(8,128)(2,1)} copy(bf16[384,2304]{1,0:T(8,128)(2,1)} %shard_map.46) | data formatting | bytes 3538944

commit v5 on v4

--- a/solution.py
+++ b/solution.py
@@ -23,8 +23,8 @@
 
 
 def kernel(
-    group, chunks, seqs, count, x_ref, freq_ref, widths_ref, seg_ref, out_ref,
-    x_held, turns, key_seg, send, held, keys, values, queries, blended, back,
+    group, chunks, seqs, count, x_ref, freq_ref, widths_ref, seg_ref, back,
+    x_held, turns, key_seg, send, held, keys, values, queries, blended,
     x_sem, in_send, in_recv, in_own, halo_send, halo_recv, back_send, back_recv, back_own,
 ):
     tok = x_ref.shape[0]
@@ -37,6 +37,15 @@
     has_right = seq < seqs - 1
     scale = math.log2(math.e) / math.sqrt(HEAD)
 
+    def partner(d):
+        place, found = 1, 0
+        while place < group:
+            found = found + lax.rem(me // place + d // place, 2) * place
+            place *= 2
+        return found
+
+    partners = range(group - 1, 0, -1)
+
     columns = (2 * D, D, 0)
 
     def x_copy(j, part):
@@ -45,14 +54,13 @@
             x_ref.at[:, pl.ds(first, span)], x_held.at[j, part], x_sem.at[j, part]
         )
 
-    for j in range(chunks):
-        for part in range(3):
-            x_copy(j, part).start()
+    for part in range(3):
+        x_copy(0, part).start()
 
     barrier = pltpu.get_barrier_semaphore()
-    for d in range(1, group):
+    for d in partners:
         pl.semaphore_signal(
-            barrier, inc=1, device_id={"head": lax.rem(me + d, group)}, device_id_type=MESH
+            barrier, inc=1, device_id={"head": partner(d)}, device_id_type=MESH
         )
 
     @pl.when(has_left)
@@ -68,7 +76,7 @@
     )
 
     def in_copy(j, d, part):
-        dest = lax.rem(me + d, group)
+        dest = partner(d)
         return pltpu.make_async_remote_copy(
             src_ref=send.at[j, dest, part],
             dst_ref=held.at[j, group + me, part],
@@ -95,7 +103,7 @@
         )
 
     def back_copy(j, d):
-        dest = lax.rem(me + d, group)
+        dest = partner(d)
         return pltpu.make_async_remote_copy(
             src_ref=blended.at[j, dest],
             dst_ref=back.at[j, me],
@@ -125,13 +133,13 @@
             send[j, z, part] = vals.astype(jnp.bfloat16)
 
     def issue(j, part):
-        for d in range(1, group):
+        for d in partners:
             in_copy(j, d, part).start()
         own_copy(j, part).start()
 
     def arrive(j, part):
         own_copy(j, part).wait()
-        for d in range(1, group):
+        for d in partners:
             in_copy(j, d, part).wait_recv()
 
     rows = tok // seg_ref.shape[1]
@@ -195,8 +203,8 @@
                 held[j, 2 * group + z] = jnp.zeros((3, HEAD, tok), jnp.bfloat16)
 
     def back_start(j, first=0, last=group):
-        for d in range(1, group):
-            dest = lax.rem(me + d, group)
+        for d in partners:
+            dest = partner(d)
 
             @pl.when(jnp.logical_and(dest >= first, dest < last))
             def _():
@@ -246,6 +254,9 @@
 
     prepare(0, 0)
     issue(0, 0)
+    for j in range(1, chunks):
+        for part in range(3):
+            x_copy(j, part).start()
     lay_out()
     for part in (1, 2):
         prepare(0, part)
@@ -313,11 +324,9 @@
 
     def finish(j, carry):
         back_own_copy(j).wait()
-        for d in range(1, group):
+        for d in partners:
             back_copy(j, d).wait_recv()
-        rows = jnp.concatenate([back[j, z] for z in range(group)], axis=0)
-        out_ref[:, pl.ds(pl.multiple_of(j * span, 128), span)] = transposed(rows)
-        for d in range(1, group):
+        for d in partners:
             for part in range(3):
                 in_copy(j, d, part).wait_send()
             back_copy(j, d).wait_send()
@@ -333,6 +342,11 @@
         return carry
 
     lax.fori_loop(0, chunks, finish, 0)
+
+
+def turned(back_ref, out_ref):
+    rows = jnp.concatenate([back_ref[0, z] for z in range(back_ref.shape[1])], axis=0)
+    out_ref[...] = transposed(rows)
 
 
 def body(projected, segment_ids, widths):
@@ -348,13 +362,13 @@
 
     vmem = pl.BlockSpec(memory_space=pltpu.VMEM)
     dma = pltpu.SemaphoreType.DMA
-    return pl.pallas_call(
+    back = pl.pallas_call(
         functools.partial(kernel, group, chunks, seqs, count),
-        out_shape=jax.ShapeDtypeStruct((tok, D), jnp.bfloat16),
+        out_shape=jax.ShapeDtypeStruct((chunks, group, HEAD, tok), jnp.bfloat16),
         in_specs=[
             pl.BlockSpec(memory_space=pl.ANY), vmem, pl.BlockSpec(memory_space=pltpu.SMEM), vmem
         ],
-        out_specs=vmem,
+        out_specs=pl.BlockSpec(memory_space=pl.ANY),
         scratch_shapes=[
             pltpu.VMEM((chunks, 3, tok, group * HEAD), jnp.bfloat16),
             pltpu.VMEM((4, QUARTER, tok), jnp.float32),
@@ -364,7 +378,6 @@
             pltpu.VMEM((3 * shard, HEAD + aug), jnp.bfloat16),
             pltpu.VMEM((HEAD + ONES, 3 * shard), jnp.bfloat16),
             pltpu.VMEM((HEAD + aug, shard), jnp.bfloat16),
-            pltpu.VMEM((chunks, group, HEAD, tok), jnp.bfloat16),
             pltpu.VMEM((chunks, group, HEAD, tok), jnp.bfloat16),
             dma((chunks, 3)),
             dma((chunks, group - 1, 3)),
@@ -383,6 +396,13 @@
             flops=4 * shard * shard * 2 * D // group, bytes_accessed=tok * D * 8, transcendentals=0
         ),
     )(projected, frequency[:, None], widths, segment_ids.reshape(-1, 128 if tok % 128 == 0 else tok))
+    return pl.pallas_call(
+        turned,
+        grid=(chunks,),
+        out_shape=jax.ShapeDtypeStruct((tok, D), jnp.bfloat16),
+        in_specs=[pl.BlockSpec((1, group, HEAD, tok), lambda j: (j, 0, 0, 0))],
+        out_specs=pl.BlockSpec((tok, group * HEAD), lambda j: (0, j)),
+    )(back)
 
 
 def solution(mesh):

time: 165 us -> 167 us (1.012)
  Pallas kernels: 162 us -> 166 us
  local copies, waits for them, and re-layouts: 2.8 us -> 0 us
    pallas_call x0 -> x1, Pallas kernels: none -> 4.93 us  [body(): pl.pallas_call(turned, grid=(chunks,), out_shape=jax.ShapeDtypeStruct((to...]
    unnamed x1 -> x0, local copies, waits for them, and re-layouts: 2.8 us -> none
where the time goes in v5:
time: 167 us; the launch traced here: 166 us
  Pallas kernels  166 us (99%)
    pallas_call x1, Pallas kernels, body(): pl.pallas_call(functools.partial(kernel, group, chunks, seqs, count), out...  161 us
    pallas_call x1, Pallas kernels, body(): pl.pallas_call(turned, grid=(chunks,), out_shape=jax.ShapeDtypeStruct((to...  4.93 us

profile of v5, /device:TPU:0, one launch (start us, length us, event | category | flops | bytes accessed | tf_op | source)
XLA Modules:
  0.0 166.3 jit_solution(3589844630467068892)
XLA Ops:
  0.0 161.3 %shard_map.46.back_ref = bf16[6,4,96,384]{3,2,1,0:T(8,128)(2,1)} custom-call(bf16[384,6912]{1,0:T(8,128)(2,1)} %x_ref.1, f32[24,1]{1,0:T(8,128)} %constant.3.freq_ref, s32[16]{0:T(128)} %widths_ref.1, s32[96,128]{1,0:T(8,128)} %bitcast.1), custom_call_target="tpu_custom_call" | custom-call | flops 10871635968 | bytes 7077888 | tf_op jit(solution)/shard_map/pallas_call | solution.py:365
  161.3 4.9 %shard_map.47 = bf16[384,2304]{1,0:T(8,128)(2,1)} custom-call(bf16[6,4,96,384]{3,2,1,0:T(8,128)(2,1)} %shard_map.46.back_ref), custom_call_target="tpu_custom_call" | custom-call | tf_op jit(solution)/shard_map/pallas_call | solution.py:399

commit v6 on v5

--- a/solution.py
+++ b/solution.py
@@ -23,8 +23,8 @@
 
 
 def kernel(
-    group, chunks, seqs, count, x_ref, freq_ref, widths_ref, seg_ref, back,
-    x_held, turns, key_seg, send, held, keys, values, queries, blended,
+    group, chunks, seqs, count, x_ref, freq_ref, widths_ref, seg_ref, out_ref,
+    x_held, turns, key_seg, send, held, keys, values, queries, blended, back,
     x_sem, in_send, in_recv, in_own, halo_send, halo_recv, back_send, back_recv, back_own,
 ):
     tok = x_ref.shape[0]
@@ -244,7 +244,7 @@
 
             top = jnp.full((1, wide), -1e30, jnp.float32)
             acc = jnp.zeros((HEAD + ONES, wide), jnp.float32)
-            top, acc = lax.fori_loop(0, group + 1, key_block, (top, acc))
+            top, acc = lax.fori_loop(0, group + 1, key_block, (top, acc), unroll=True)
             mean = (acc[:HEAD] / acc[HEAD:HEAD + 1]).astype(jnp.bfloat16)
             blended[j, 2 * i] = mean[:, :tok]
             blended[j, 2 * i + 1] = mean[:, tok:]
@@ -326,6 +326,8 @@
         back_own_copy(j).wait()
         for d in partners:
             back_copy(j, d).wait_recv()
+        cols = transposed(jnp.concatenate([back[j, z] for z in range(group)], axis=0))
+        out_ref[:, pl.ds(pl.multiple_of(j * span, 128), span)] = cols
         for d in partners:
             for part in range(3):
                 in_copy(j, d, part).wait_send()
@@ -342,11 +344,6 @@
         return carry
 
     lax.fori_loop(0, chunks, finish, 0)
-
-
-def turned(back_ref, out_ref):
-    rows = jnp.concatenate([back_ref[0, z] for z in range(back_ref.shape[1])], axis=0)
-    out_ref[...] = transposed(rows)
 
 
 def body(projected, segment_ids, widths):
@@ -362,13 +359,13 @@
 
     vmem = pl.BlockSpec(memory_space=pltpu.VMEM)
     dma = pltpu.SemaphoreType.DMA
-    back = pl.pallas_call(
+    return pl.pallas_call(
         functools.partial(kernel, group, chunks, seqs, count),
-        out_shape=jax.ShapeDtypeStruct((chunks, group, HEAD, tok), jnp.bfloat16),
+        out_shape=jax.ShapeDtypeStruct((tok, D), jnp.bfloat16),
         in_specs=[
             pl.BlockSpec(memory_space=pl.ANY), vmem, pl.BlockSpec(memory_space=pltpu.SMEM), vmem
         ],
-        out_specs=pl.BlockSpec(memory_space=pl.ANY),
+        out_specs=vmem,
         scratch_shapes=[
             pltpu.VMEM((chunks, 3, tok, group * HEAD), jnp.bfloat16),
             pltpu.VMEM((4, QUARTER, tok), jnp.float32),
@@ -378,6 +375,7 @@
             pltpu.VMEM((3 * shard, HEAD + aug), jnp.bfloat16),
             pltpu.VMEM((HEAD + ONES, 3 * shard), jnp.bfloat16),
             pltpu.VMEM((HEAD + aug, shard), jnp.bfloat16),
+            pltpu.VMEM((chunks, group, HEAD, tok), jnp.bfloat16),
             pltpu.VMEM((chunks, group, HEAD, tok), jnp.bfloat16),
             dma((chunks, 3)),
             dma((chunks, group - 1, 3)),
@@ -396,13 +394,6 @@
             flops=4 * shard * shard * 2 * D // group, bytes_accessed=tok * D * 8, transcendentals=0
         ),
     )(projected, frequency[:, None], widths, segment_ids.reshape(-1, 128 if tok % 128 == 0 else tok))
-    return pl.pallas_call(
-        turned,
-        grid=(chunks,),
-        out_shape=jax.ShapeDtypeStruct((tok, D), jnp.bfloat16),
-        in_specs=[pl.BlockSpec((1, group, HEAD, tok), lambda j: (j, 0, 0, 0))],
-        out_specs=pl.BlockSpec((tok, group * HEAD), lambda j: (0, j)),
-    )(back)
 
 
 def solution(mesh):

time: 167 us -> 166 us (level)
  Pallas kernels: 166 us -> 162 us
  local copies, waits for them, and re-layouts: 0 us -> 2.8 us
    pallas_call x1 -> x0, Pallas kernels: 4.93 us -> none  [body(): pl.pallas_call(turned, grid=(chunks,), out_shape=jax.ShapeDtypeStruct((to...]
    unnamed x0 -> x1, local copies, waits for them, and re-layouts: none -> 2.8 us
where the time goes in v6:
time: 166 us; the launch traced here: 165 us
  Pallas kernels  162 us (98%)
  local copies, waits for them, and re-layouts  2.8 us (2%)
    pallas_call x1, Pallas kernels, body(): pl.pallas_call(functools.partial(kernel, group, chunks, seqs, count), out...  162 us

profile of v6, /device:TPU:0, one launch (start us, length us, event | category | flops | bytes accessed | tf_op | source)
XLA Modules:
  0.0 165.3 jit_solution(15604983001523145530)
XLA Ops:
  0.0 162.5 %shard_map.46 = bf16[384,2304]{1,0:T(8,128)(2,1)} custom-call(bf16[384,6912]{1,0:T(8,128)(2,1)} %x_ref.1, f32[24,1]{1,0:T(8,128)} %constant.3.freq_ref, s32[16]{0:T(128)} %widths_ref.1, s32[96,128]{1,0:T(8,128)} %bitcast.1), custom_call_target="tpu_custom_call" | custom-call | flops 10871635968 | bytes 7077888 | tf_op jit(solution)/shard_map/pallas_call | solution.py:362
  162.5 2.8 %copy.6 = bf16[384,2304]{1,0:T(8,128)(2,1)} copy(bf16[384,2304]{1,0:T(8,128)(2,1)} %shard_map.46) | data formatting | bytes 3538944
